TPU v7x, 32 devices: a whole 2x2x4 slice. The times are simulated.
32 devices in a mesh: gx: 4 (over y, x), gy: 2 (over core), gz: 4 (over z).
Axes of the slice: x: 2, y: 2, z: 4, core: 2. Of those that a mesh axis runs over, the one named last changes fastest.
Arguments:
- velocity: float32 [3, 32, 16, 512], P(None, 'gx', 'gy', 'gz'), may hold values from -6 to 6
- features: bfloat16 [16, 32, 16, 512], P(None, 'gx', 'gy', 'gz'), may hold values from -6 to 6
- density: float32 [32, 16, 512], P('gx', 'gy', 'gz'), may hold values from 0.5 to 2
- target: float32 [3, 32, 16, 512], P(None, 'gx', 'gy', 'gz'), may hold values from -6 to 6
- weight_in: bfloat16 [16, 64], replicated, may hold values from -1.5 to 1.5
- bias_in: float32 [64], replicated, may hold values from -3 to 3
- weight_out: bfloat16 [64, 3], replicated, may hold values from -0.75 to 0.75
- open_faces: int32 [6], replicated, may hold values from 0 to 1
Outputs:
- new_velocity: float32 [3, 32, 16, 512], P(None, 'gx', 'gy', 'gz')
- grad_weight_in: float32 [16, 64], replicated
- grad_bias_in: float32 [64], replicated
- grad_weight_out: float32 [64, 3], replicated
Inputs may be any that keep to these rules, and one draw needn't show every extreme that they name: `open_faces`: entries in the order low first, high first, low second, high second, low third, high third face; 1 marks an open face (pressure zero beyond it), 0 a wall.
All inputs are finite; a program needn't handle non-finite values.
Results may differ from a plain program's by a relative error of at most 0.0012.
Values sent between devices are 32-bit elements; how exact they have to be, the bound alone decides.
A program may use at most 128 MiB of HBM per device.

v0:
```python
import jax
import jax.numpy as jnp
from jax import lax
from jax.sharding import PartitionSpec as P

SWEEPS = 3
COARSE_SWEEPS = 6


RELAXATION = 0.8
MASS_SHIFT = 0.05
SHAPES = ((-1, 1, 1), (1, -1, 1), (1, 1, -1))


def with_halo(shard, sides, width):
    for axis, dim in sides:
        count, length = (lax.axis_size(axis), shard.shape[dim])
        up = [(i, (i + 1) % count) for i in range(count - 1)]
        down = [(j, i) for i, j in up]
        last = lax.slice_in_dim(shard, length - width, length, axis=dim)
        leading = lax.slice_in_dim(shard, 0, width, axis=dim)
        before = lax.ppermute(last, axis, up)
        after = lax.ppermute(leading, axis, down)
        shard = jnp.concatenate([before, shard, after], axis=dim)
    return shard


def zero_padded(field):
    return jnp.pad(field, 1)


def halo_padded(field):
    return with_halo(field, (("gx", 0), ("gy", 1), ("gz", 2)), 1)


def deep_padded(field):
    return with_halo(field, (("gx", 0), ("gy", 1), ("gz", 2)), SWEEPS)


def deep_coefs(level_data):
    stacked = jnp.stack(list(level_data[1]) + list(level_data[2]) + [level_data[3]])
    extended = with_halo(stacked, (("gx", 1), ("gy", 2), ("gz", 3)), SWEEPS)
    diagonal = extended[6]
    safe_diagonal = jnp.where(diagonal > 0.0, diagonal, jnp.float32(1.0))
    return (
        (extended[0], extended[1], extended[2]),
        (extended[3], extended[4], extended[5]),
        diagonal,
        safe_diagonal,
    )


def trimmed(field, margin):
    span_first, span_second, span_third = field.shape
    return field[
        margin : span_first - margin, margin : span_second - margin, margin : span_third - margin
    ]


def apply_inner(iterate, extended, width):
    margin = SWEEPS - (width - 1)
    uppers = tuple((trimmed(extended[0][direction], margin) for direction in range(3)))
    lowers = tuple((trimmed(extended[1][direction], margin) for direction in range(3)))
    diagonal = trimmed(extended[2], margin)
    summed = neighbour_sum(iterate, uppers, lowers)
    return diagonal * iterate[1:-1, 1:-1, 1:-1] - summed


def sweep_inner(iterate, source_ext, extended, width):
    margin = SWEEPS - (width - 1)
    residue = trimmed(source_ext, margin) - apply_inner(iterate, extended, width)
    return iterate[1:-1, 1:-1, 1:-1] + RELAXATION * residue / trimmed(extended[3], margin)


def gather_whole(coarse_piece):
    span_first, span_second, span_third = coarse_piece.shape
    flattened = coarse_piece.reshape(1, span_first * span_second * span_third)
    gathered = lax.all_gather(flattened, ("gx", "gy", "gz"), axis=0, tiled=True)
    blocks = gathered.reshape(
        lax.axis_size("gx"),
        lax.axis_size("gy"),
        lax.axis_size("gz"),
        span_first,
        span_second,
        span_third,
    )
    return blocks.transpose(0, 3, 1, 4, 2, 5).reshape(
        lax.axis_size("gx") * span_first,
        lax.axis_size("gy") * span_second,
        lax.axis_size("gz") * span_third,
    )


def edge_factors(length, offset, whole_length, lower_flag, upper_flag):
    position = jnp.arange(length, dtype=jnp.int32) + offset
    lower = jnp.where(position == 0, lower_flag.astype(jnp.float32), jnp.float32(1.0))
    upper = jnp.where(
        position == whole_length - 1, upper_flag.astype(jnp.float32), jnp.float32(1.0)
    )
    return (lower, upper)


def coefficients(padded_density, factors, weight):
    centre = padded_density[1:-1, 1:-1, 1:-1]
    following = (
        padded_density[2:, 1:-1, 1:-1],
        padded_density[1:-1, 2:, 1:-1],
        padded_density[1:-1, 1:-1, 2:],
    )
    preceding = (
        padded_density[:-2, 1:-1, 1:-1],
        padded_density[1:-1, :-2, 1:-1],
        padded_density[1:-1, 1:-1, :-2],
    )
    upper_coefs = tuple(
        (
            weight
            * 2.0
            / (centre + following[direction])
            * factors[direction][1].reshape(SHAPES[direction])
            for direction in range(3)
        )
    )
    lower_coefs = tuple(
        (
            weight
            * 2.0
            / (centre + preceding[direction])
            * factors[direction][0].reshape(SHAPES[direction])
            for direction in range(3)
        )
    )
    diagonal = (
        MASS_SHIFT
        + upper_coefs[0]
        + lower_coefs[0]
        + upper_coefs[1]
        + lower_coefs[1]
        + upper_coefs[2]
        + lower_coefs[2]
    )
    return (upper_coefs, lower_coefs, diagonal)


def neighbour_sum(padded_field, upper_coefs, lower_coefs):
    summed = (
        upper_coefs[0] * padded_field[2:, 1:-1, 1:-1]
        + lower_coefs[0] * padded_field[:-2, 1:-1, 1:-1]
    )
    summed = (
        summed
        + upper_coefs[1] * padded_field[1:-1, 2:, 1:-1]
        + lower_coefs[1] * padded_field[1:-1, :-2, 1:-1]
    )
    summed = (
        summed
        + upper_coefs[2] * padded_field[1:-1, 1:-1, 2:]
        + lower_coefs[2] * padded_field[1:-1, 1:-1, :-2]
    )
    return summed


def apply_level(field, level_data):
    return level_data[3] * field - neighbour_sum(level_data[0](field), level_data[1], level_data[2])


def smooth_once(iterate, source, level_data):
    return iterate + RELAXATION * (source - apply_level(iterate, level_data)) / level_data[3]


def relax_from_zero(source, level_data, sweeps_count):
    iterate = RELAXATION * source / level_data[3]
    for repeat in range(sweeps_count - 1):
        iterate = smooth_once(iterate, source, level_data)
    return iterate


def restrict(field):
    span_first, span_second, span_third = field.shape
    return field.reshape(span_first // 2, 2, span_second // 2, 2, span_third // 2, 2).mean(
        axis=(1, 3, 5)
    )


def prolong(field):
    span_first, span_second, span_third = field.shape
    spread = jnp.broadcast_to(
        field[:, None, :, None, :, None], (span_first, 2, span_second, 2, span_third, 2)
    )
    return spread.reshape(2 * span_first, 2 * span_second, 2 * span_third)


def deep_cycle(source, extended_levels, coarse_solve):
    extended = extended_levels[0]
    source_ext = deep_padded(source)
    iterate = RELAXATION * source_ext / extended[3]
    width = SWEEPS
    for repeat in range(SWEEPS - 1):
        iterate = sweep_inner(iterate, source_ext, extended, width)
        width = width - 1
    margin = SWEEPS - (width - 1)
    residue = trimmed(source_ext, margin) - apply_inner(iterate, extended, width)
    iterate = trimmed(iterate, width)
    if len(extended_levels) > 1:
        correction = deep_cycle(restrict(residue), extended_levels[1:], coarse_solve)
    else:
        correction = coarse_solve(restrict(residue))
    iterate = deep_padded(iterate + prolong(correction))
    width = SWEEPS
    for repeat in range(SWEEPS):
        iterate = sweep_inner(iterate, source_ext, extended, width)
        width = width - 1
    return iterate


def deep_solve(source, levels, extended_levels, coarse_solve):
    iterate = deep_cycle(source, extended_levels, coarse_solve)
    iterate = iterate + deep_cycle(
        source - apply_level(iterate, levels[0]), extended_levels, coarse_solve
    )
    return iterate


def divergence(fluxes, padder):
    first = padder(fluxes[0])[:-2, 1:-1, 1:-1]
    second = padder(fluxes[1])[1:-1, :-2, 1:-1]
    third = padder(fluxes[2])[1:-1, 1:-1, :-2]
    return fluxes[0] - first + (fluxes[1] - second) + (fluxes[2] - third)


def upward_differences(field, padder):
    padded = padder(field)
    return (
        padded[2:, 1:-1, 1:-1] - field,
        padded[1:-1, 2:, 1:-1] - field,
        padded[1:-1, 1:-1, 2:] - field,
    )


def closure_plane(feature_plane, weight_in, bias_in, weight_out):
    columns = feature_plane.reshape(feature_plane.shape[0], -1)
    before = jnp.dot(weight_in.T, columns, preferred_element_type=jnp.float32) + bias_in[:, None]
    gate = jax.nn.sigmoid(before)
    hidden = (before * gate).astype(jnp.bfloat16)
    output = jnp.dot(weight_out.T, hidden, preferred_element_type=jnp.float32)
    return output.reshape((3,) + feature_plane.shape[1:])


def closure_field(features, weight_in, bias_in, weight_out):

    def one_plane(index):
        feature_plane = lax.dynamic_index_in_dim(features, index, 1, keepdims=False)
        return closure_plane(feature_plane, weight_in, bias_in, weight_out)

    stacked = lax.map(one_plane, jnp.arange(features.shape[1], dtype=jnp.int32))
    return jnp.moveaxis(stacked, 0, 1)


def gradient_plane(totals, feature_plane, grad_plane, weight_in, bias_in, weight_out):
    columns = feature_plane.reshape(feature_plane.shape[0], -1)
    before = jnp.dot(weight_in.T, columns, preferred_element_type=jnp.float32) + bias_in[:, None]
    gate = jax.nn.sigmoid(before)
    hidden = (before * gate).astype(jnp.bfloat16)
    upstream = grad_plane.reshape(3, -1).astype(jnp.bfloat16)
    grad_out = lax.dot_general(
        hidden, upstream, (((1,), (1,)), ((), ())), preferred_element_type=jnp.float32
    )
    grad_hidden = jnp.dot(weight_out, upstream, preferred_element_type=jnp.float32)
    grad_before = grad_hidden * (gate * (1.0 + before * (1.0 - gate)))
    grad_bias = jnp.sum(grad_before, axis=1)
    grad_in = lax.dot_general(
        columns,
        grad_before.astype(jnp.bfloat16),
        (((1,), (1,)), ((), ())),
        preferred_element_type=jnp.float32,
    )
    return (totals[0] + grad_in, totals[1] + grad_bias, totals[2] + grad_out)


def closure_gradients(features, grad_correction, weight_in, bias_in, weight_out):

    def step_plane(totals, index):
        feature_plane = lax.dynamic_index_in_dim(features, index, 1, keepdims=False)
        grad_plane = lax.dynamic_index_in_dim(grad_correction, index, 1, keepdims=False)
        return (
            gradient_plane(totals, feature_plane, grad_plane, weight_in, bias_in, weight_out),
            None,
        )

    start = (
        jnp.zeros(weight_in.shape, jnp.float32),
        jnp.zeros(bias_in.shape, jnp.float32),
        jnp.zeros(weight_out.shape, jnp.float32),
    )
    totals, unused = lax.scan(step_plane, start, jnp.arange(features.shape[1], dtype=jnp.int32))
    return totals


def training_step(
    velocity,
    features,
    target,
    weight_in,
    bias_in,
    weight_out,
    levels,
    solver,
    fine_factors,
    cells_total,
):
    padder = levels[0][0]
    upper_coefs = levels[0][1]
    outlets = tuple(
        (fine_factors[direction][1].reshape(SHAPES[direction]) for direction in range(3))
    )
    correction = closure_field(features, weight_in, bias_in, weight_out)
    fluxes = tuple(
        (
            (velocity[direction] + correction[direction]) * outlets[direction]
            for direction in range(3)
        )
    )
    source = -divergence(fluxes, padder)
    pressure = solver(source)
    rises = upward_differences(pressure, padder)
    new_velocity = jnp.stack(
        [fluxes[direction] - upper_coefs[direction] * rises[direction] for direction in range(3)]
    )
    misfit = (new_velocity - target) / cells_total
    weighted = tuple((upper_coefs[direction] * misfit[direction] for direction in range(3)))
    grad_pressure = divergence(weighted, padder)
    grad_source = solver(grad_pressure)
    drops = upward_differences(grad_source, padder)
    grad_correction = jnp.stack(
        [(misfit[direction] + drops[direction]) * outlets[direction] for direction in range(3)]
    )
    totals = closure_gradients(features, grad_correction, weight_in, bias_in, weight_out)
    return (new_velocity, totals)


def per_device(velocity, features, density, target, weight_in, bias_in, weight_out, open_faces):
    counts = (lax.axis_size("gx"), lax.axis_size("gy"), lax.axis_size("gz"))
    indices = (lax.axis_index("gx"), lax.axis_index("gy"), lax.axis_index("gz"))

    def level_factors(shape_now):
        return tuple(
            (
                edge_factors(
                    shape_now[direction],
                    indices[direction] * shape_now[direction],
                    shape_now[direction] * counts[direction],
                    open_faces[2 * direction],
                    open_faces[2 * direction + 1],
                )
                for direction in range(3)
            )
        )

    def make_level(level_density, weight):
        upper_coefs, lower_coefs, diagonal = coefficients(
            halo_padded(level_density), level_factors(level_density.shape), weight
        )
        return (halo_padded, upper_coefs, lower_coefs, diagonal)

    density_one = restrict(density)
    density_two = restrict(density_one)
    levels = (make_level(density, 1.0), make_level(density_one, 0.25))
    whole_density = gather_whole(density_two)
    whole_factors = tuple(
        (
            edge_factors(
                whole_density.shape[direction],
                0,
                whole_density.shape[direction],
                open_faces[2 * direction],
                open_faces[2 * direction + 1],
            )
            for direction in range(3)
        )
    )
    whole_upper, whole_lower, whole_diagonal = coefficients(
        zero_padded(whole_density), whole_factors, 0.0625
    )
    coarse_level = (zero_padded, whole_upper, whole_lower, whole_diagonal)

    def coarse_solve(source):
        whole_source = gather_whole(source)
        whole_iterate = relax_from_zero(whole_source, coarse_level, COARSE_SWEEPS)
        starts = tuple((indices[direction] * source.shape[direction] for direction in range(3)))
        return lax.dynamic_slice(whole_iterate, starts, source.shape)

    extended_levels = tuple((deep_coefs(level_data) for level_data in levels))

    def solver(source):
        return deep_solve(source, levels, extended_levels, coarse_solve)

    cells_total = density.size * counts[0] * counts[1] * counts[2]
    new_velocity, totals = training_step(
        velocity,
        features,
        target,
        weight_in,
        bias_in,
        weight_out,
        levels,
        solver,
        level_factors(density.shape),
        cells_total,
    )
    summed = lax.psum((totals[0], totals[1], totals[2]), ("gx", "gy", "gz"))
    return (new_velocity, summed[0], summed[1], summed[2])


def solution(mesh):
    in_specs = (
        P(None, "gx", "gy", "gz"),
        P(None, "gx", "gy", "gz"),
        P("gx", "gy", "gz"),
        P(None, "gx", "gy", "gz"),
        P(),
        P(),
        P(),
        P(),
    )
    out_specs = (P(None, "gx", "gy", "gz"), P(), P(), P())
    return jax.shard_map(
        per_device, mesh=mesh, in_specs=in_specs, out_specs=out_specs, check_vma=False
    )
```

profile of v0, /device:TPU:0, one launch (start us, length us, event | category | flops | bytes accessed | tf_op | source)
XLA Modules:
  0.0 1196.4 jit_solution(14311903983373155404)
XLA Ops:
  2.6 5.5 collective-permute-start.16
  11.6 34.6 %while.25 = (s32[]{:T(128)}, f32[8,3,8,128]{3,2,0,1:T(8,128)S(1)}, s32[8]{0:T(128)S(1)}, bf16[16,8,8,128]{3,2,1,0:T(8,128)(2,1)}, bf16[16,64]{1,0:T(8,128)(2,1)}...) while((s32[]{:T(128)}, f32[8,3,8,128]{3,2,0,1:T(8,128)S(1)}, ...), condition=%wide.region_1.0_spmd, body=%wide.region_0.0_spmd.sunk | while | flops 2883589 | bytes 142107 | solution.py:255
  46.3 4.8 collective-permute-start.5
  86.8 4.9 collective-permute-start.1
  91.8 4.8 collective-permute-start.39
  113.9 4.6 collective-permute-start.20
  118.6 4.5 collective-permute-start.10
  125.0 4.6 collective-permute-start.21
  152.2 4.6 collective-permute-start.25
  160.4 5.2 collective-permute-start.43
  190.9 67.1 %all-gather.1 = f32[32,1,128]{2,1,0:T(1,128)S(1)} all-gather(f32[1,1,128]{2,1,0:T(1,128)S(1)} %copy-done.119), channel_id=1, replica_groups=mesh['gx'=4,'gy'=2,'gz'=4] {'gx','gy','gz'}, dimensions={0}, use_global_device_ids=true | all-gather | bytes 16896 | tf_op jit(solution)/shard_map/all_gather | solution.py:78
  278.1 4.6 collective-permute-done.32
  287.3 63.2 %all-gather = f32[32,1,128]{2,1,0:T(1,128)S(1)} all-gather(f32[1,1,128]{2,1,0:T(1,128)S(1)} %reshape.328), channel_id=1, replica_groups=mesh['gx'=4,'gy'=2,'gz'=4] {'gx','gy','gz'}, dimensions={0}, use_global_device_ids=true | all-gather | bytes 16896 | tf_op jit(solution)/shard_map/all_gather | solution.py:78
  364.6 7.6 collective-permute-done.46
  396.9 4.8 collective-permute-start.51
  424.1 4.5 collective-permute-start.58
  436.5 4.6 collective-permute-start.62
  448.9 4.9 collective-permute-done.64
  480.2 4.8 collective-permute-start.69
  515.0 66.2 %all-gather.2 = f32[32,1,128]{2,1,0:T(1,128)} all-gather(f32[1,1,128]{2,1,0:T(1,128)} %reshape.332), channel_id=1, replica_groups=mesh['gx'=4,'gy'=2,'gz'=4] {'gx','gy','gz'}, dimensions={0}, use_global_device_ids=true | all-gather | bytes 16896 | tf_op jit(solution)/shard_map/all_gather | solution.py:78
  666.0 5.2 collective-permute-done.91
  677.5 5.2 collective-permute-start.93
  684.1 5.4 collective-permute-start.92
  699.7 4.8 collective-permute-start.101
  769.4 66.1 %all-gather.3 = f32[32,1,128]{2,1,0:T(1,128)} all-gather(f32[1,1,128]{2,1,0:T(1,128)} %reshape.334), channel_id=1, replica_groups=mesh['gx'=4,'gy'=2,'gz'=4] {'gx','gy','gz'}, dimensions={0}, use_global_device_ids=true | all-gather | bytes 16896 | tf_op jit(solution)/shard_map/all_gather | solution.py:78
  920.1 4.6 collective-permute-start.130
  932.5 4.9 collective-permute-done.132
  960.6 4.8 collective-permute-start.137
  986.3 63.2 %all-gather.4 = f32[32,1,128]{2,1,0:T(1,128)S(1)} all-gather(f32[1,1,128]{2,1,0:T(1,128)S(1)} %reshape.336), channel_id=1, replica_groups=mesh['gx'=4,'gy'=2,'gz'=4] {'gx','gy','gz'}, dimensions={0}, use_global_device_ids=true | all-gather | bytes 16896 | tf_op jit(solution)/shard_map/all_gather | solution.py:78
  1117.1 5.3 collective-permute-done.159
  1122.5 34.0 %while.26 = (s32[]{:T(128)}, f32[16,64]{1,0:T(8,128)S(1)}, f32[64]{0:T(128)S(1)}, f32[64,3]{0,1:T(4,128)S(1)}, s32[8]{0:T(128)S(1)}, /*index=5*/bf16[16,8,8,128]...) while((s32[]{:T(128)}, f32[16,64]{1,0:T(8,128)S(1)}, ...), condition=%wide.region_14.15_spmd.clone, body=%wide.region_12.14_spmd.clone.sunk | while | flops 6031814 | bytes 1217855 | solution.py:295
  1156.5 39.7 %all-reduce.21 = (f32[16,64]{1,0:T(8,128)}, f32[64]{0:T(128)}, f32[64,3]{0,1:T(4,128)}) all-reduce(f32[16,64]{1,0:T(8,128)S(1)} %get-tuple-element.96, f32[64]{0:T(128)S(1)} %get-tuple-element.97, f32[64,3]{0,1:T(4,128)S(1)} %get-tuple-element.98), channel_id=1, replica_groups=mesh['gx'=4,'gy'=2,'gz'=4] {'gx','gy','gz'}, use_global_device_ids=true, to_apply=%region_15.16 | all-reduce | flops 1280 | bytes 10240 | tf_op jit(solution)/shard_map/psum | solution.py:410
  (994 shorter events, 671.3 us)
Async XLA Ops:
  1.3 85.4 %collective-permute-start = (f32[1,8,128]{2,1,0:T(8,128)S(1)}, f32[1,8,128]{2,1,0:T(8,128)S(1)}, u32[]{:S(2)}, u32[]{:S(2)}) collective-permute-start(f32[1,8,128]{2,1,0:T(8,128)S(1)} %get-tuple-element.349), channel_id=1, source_target_pairs={{8,0},{16,8},{24,16},{9,1},{17,9},{25,17},{10,2},{18,10},{26,18},{... | collective-permute-start | bytes 12296 | tf_op jit(solution)/shard_map/ppermute | solution.py:23
  2.6 82.8 %collective-permute-start.16 = (f32[1,8,128]{2,1,0:T(8,128)S(1)}, f32[1,8,128]{2,1,0:T(8,128)S(1)}, u32[]{:S(2)}, u32[]{:S(2)}) collective-permute-start(f32[1,8,128]{2,1,0:T(8,128)S(1)} %get-tuple-element.348), channel_id=1, source_target_pairs={{0,8},{8,16},{16,24},{1,9},{9,17},{17,25},{2,10},{10,18},{18,26},{... | collective-permute-start | bytes 12296 | tf_op jit(solution)/shard_map/ppermute | solution.py:22
  46.3 45.5 %collective-permute-start.5 = (f32[1,8,128]{2,1,0:T(8,128)S(1)}, f32[1,8,128]{2,1,0:T(8,128)S(1)}, u32[]{:S(2)}, u32[]{:S(2)}) collective-permute-start(f32[1,8,128]{2,1,0:T(8,128)S(1)} %get-tuple-element.346), channel_id=1, source_target_pairs={{0,8},{8,16},{16,24},{1,9},{9,17},{17,25},{2,10},{10,18},{18,26},{... | collective-permute-start | bytes 12296 | tf_op jit(solution)/shard_map/ppermute | solution.py:22
  53.5 10.6 collective-permute-start.33
  54.8 9.3 collective-permute-start.34
  68.6 28.1 %collective-permute-start.6 = (f32[1,8,128]{2,1,0:T(8,128)S(1)}, f32[1,8,128]{2,1,0:T(8,128)S(1)}, u32[]{:S(2)}, u32[]{:S(2)}) collective-permute-start(f32[1,8,128]{2,1,0:T(8,128)S(1)} %get-tuple-element.347), channel_id=1, source_target_pairs={{8,0},{16,8},{24,16},{9,1},{17,9},{25,17},{10,2},{18,10},{26,18},{... | collective-permute-start | bytes 12296 | tf_op jit(solution)/shard_map/ppermute | solution.py:23
  80.7 17.3 %collective-permute-start.2 = (f32[1,8,128]{2,1,0:T(8,128)S(1)}, f32[1,8,128]{2,1,0:T(8,128)S(1)}, u32[]{:S(2)}, u32[]{:S(2)}) collective-permute-start(f32[1,8,128]{2,1,0:T(8,128)S(1)} %get-tuple-element.344), channel_id=1, source_target_pairs={{0,8},{8,16},{16,24},{1,9},{9,17},{17,25},{2,10},{10,18},{18,26},{... | collective-permute-start | bytes 12296 | tf_op jit(solution)/shard_map/ppermute | solution.py:22
  85.4 13.9 %collective-permute-start.3 = (f32[1,8,128]{2,1,0:T(8,128)S(1)}, f32[1,8,128]{2,1,0:T(8,128)S(1)}, u32[]{:S(2)}, u32[]{:S(2)}) collective-permute-start(f32[1,8,128]{2,1,0:T(8,128)S(1)} %get-tuple-element.345), channel_id=1, source_target_pairs={{8,0},{16,8},{24,16},{9,1},{17,9},{25,17},{10,2},{18,10},{26,18},{... | collective-permute-start | bytes 12296 | tf_op jit(solution)/shard_map/ppermute | solution.py:23
  86.8 25.8 %collective-permute-start.1 = (f32[1,8,128]{2,1,0:T(8,128)S(1)}, f32[1,8,128]{2,1,0:T(8,128)S(1)}, u32[]{:S(2)}, u32[]{:S(2)}) collective-permute-start(f32[1,8,128]{2,1,0:T(8,128)S(1)} %slice.3468), channel_id=1, source_target_pairs={{0,8},{8,16},{16,24},{1,9},{9,17},{17,25},{2,10},{10,18},{18,26},{... | collective-permute-start | bytes 12296 | tf_op jit(solution)/shard_map/ppermute | solution.py:22
  91.8 40.4 %collective-permute-start.39 = (f32[7,3,4,64]{3,2,1,0:T(4,128)S(1)}, f32[7,3,4,64]{3,2,1,0:T(4,128)S(1)}, u32[]{:S(2)}, u32[]{:S(2)}) collective-permute-start(f32[7,3,4,64]{3,2,1,0:T(4,128)S(1)} %get-tuple-element.298), channel_id=1, source_target_pairs={{0,8},{8,16},{16,24},{1,9},{9,17},{17,25},{2,10},{10,18},{18,26},{... | collective-permute-start | bytes 64520 | tf_op jit(solution)/shard_map/ppermute | solution.py:22
  96.7 36.9 %collective-permute-start.40 = (f32[7,3,4,64]{3,2,1,0:T(4,128)S(1)}, f32[7,3,4,64]{3,2,1,0:T(4,128)S(1)}, u32[]{:S(2)}, u32[]{:S(2)}) collective-permute-start(f32[7,3,4,64]{3,2,1,0:T(4,128)S(1)} %get-tuple-element.299), channel_id=1, source_target_pairs={{8,0},{16,8},{24,16},{9,1},{17,9},{25,17},{10,2},{18,10},{26,18},{... | collective-permute-start | bytes 64520 | tf_op jit(solution)/shard_map/ppermute | solution.py:23
  108.3 10.2 collective-permute-start.9
  112.6 10.6 collective-permute-start.19
  113.9 10.9 collective-permute-start.20
  118.6 11.0 collective-permute-start.10
  125.0 13.1 %collective-permute-start.21 = (f32[7,3,8,128]{3,2,1,0:T(8,128)S(1)}, f32[7,3,8,128]{3,2,1,0:T(8,128)S(1)}, u32[]{:S(2)}, u32[]{:S(2)}) collective-permute-start(f32[7,3,8,128]{3,2,1,0:T(8,128)S(1)} %get-tuple-element.231), channel_id=1, source_target_pairs={{0,8},{8,16},{16,24},{1,9},{9,17},{17,25},{2,10},{10,18},{18,26},{... | collective-permute-start | bytes 258056 | tf_op jit(solution)/shard_map/ppermute | solution.py:22
  133.7 14.3 %collective-permute-start.41 = (f32[7,10,3,64]{3,2,1,0:T(4,128)S(1)}, f32[7,10,3,64]{3,2,1,0:T(4,128)S(1)}, u32[]{:S(2)}, u32[]{:S(2)}) collective-permute-start(f32[7,10,3,64]{3,2,1,0:T(4,128)S(1)} %get-tuple-element.238), channel_id=1, source_target_pairs={{0,4},{1,5},{2,6},{3,7},{8,12},{9,13},{10,14},{11,15},{16,20},{17,... | collective-permute-start | bytes 161288 | tf_op jit(solution)/shard_map/ppermute | solution.py:22
  136.8 12.6 %collective-permute-start.42 = (f32[7,10,3,64]{3,2,1,0:T(4,128)S(1)}, f32[7,10,3,64]{3,2,1,0:T(4,128)S(1)}, u32[]{:S(2)}, u32[]{:S(2)}) collective-permute-start(f32[7,10,3,64]{3,2,1,0:T(4,128)S(1)} %get-tuple-element.239), channel_id=1, source_target_pairs={{4,0},{5,1},{6,2},{7,3},{12,8},{13,9},{14,10},{15,11},{20,16},{21,... | collective-permute-start | bytes 161288 | tf_op jit(solution)/shard_map/ppermute | solution.py:23
  138.8 10.7 collective-permute-start.23
  144.0 29.6 %collective-permute-start.14 = (f32[14,14,3]{2,1,0:T(8,128)}, f32[14,14,3]{2,1,0:T(8,128)}, u32[]{:S(2)}, u32[]{:S(2)}) collective-permute-start(f32[14,14,3]{2,1,0:T(8,128)} %get-tuple-element.255), channel_id=1, source_target_pairs={{0,1},{1,2},{2,3},{4,5},{5,6},{6,7},{8,9},{9,10},{10,11},{12,13},{... | collective-permute-start | bytes 7064 | tf_op jit(solution)/shard_map/ppermute | solution.py:22
  148.1 25.5 %collective-permute-start.15 = (f32[14,14,3]{2,1,0:T(8,128)}, f32[14,14,3]{2,1,0:T(8,128)}, u32[]{:S(2)}, u32[]{:S(2)}) collective-permute-start(f32[14,14,3]{2,1,0:T(8,128)} %get-tuple-element.256), channel_id=1, source_target_pairs={{1,0},{2,1},{3,2},{5,4},{6,5},{7,6},{9,8},{10,9},{11,10},{13,12},{... | collective-permute-start | bytes 7064 | tf_op jit(solution)/shard_map/ppermute | solution.py:23
  152.2 14.6 %collective-permute-start.25 = (f32[7,14,14,3]{2,1,3,0:T(8,128)S(1)}, f32[7,14,14,3]{2,1,3,0:T(8,128)S(1)}, u32[]{:S(2)}, u32[]{:S(2)}) collective-permute-start(f32[7,14,14,3]{2,1,3,0:T(8,128)S(1)} %copy.24), channel_id=1, source_target_pairs={{0,1},{1,2},{2,3},{4,5},{5,6},{6,7},{8,9},{9,10},{10,11},{12,13},{... | collective-permute-start | bytes 49400 | tf_op jit(solution)/shard_map/ppermute | solution.py:22
  157.6 11.7 collective-permute-start.26
  160.4 102.7 %collective-permute-start.43 = (f32[7,10,10,3]{2,0,3,1:T(8,128)}, f32[7,10,10,3]{2,0,3,1:T(8,128)}, u32[]{:S(2)}, u32[]{:S(2)}) collective-permute-start(f32[7,10,10,3]{2,0,3,1:T(8,128)} %copy.28), channel_id=1, source_target_pairs={{0,1},{1,2},{2,3},{4,5},{5,6},{6,7},{8,9},{9,10},{10,11},{12,13},{... | collective-permute-start | bytes 25208 | tf_op jit(solution)/shard_map/ppermute | solution.py:22
  166.8 98.5 %collective-permute-start.44 = (f32[7,10,10,3]{2,0,3,1:T(8,128)}, f32[7,10,10,3]{2,0,3,1:T(8,128)}, u32[]{:S(2)}, u32[]{:S(2)}) collective-permute-start(f32[7,10,10,3]{2,0,3,1:T(8,128)} %copy.29), channel_id=1, source_target_pairs={{1,0},{2,1},{3,2},{5,4},{6,5},{7,6},{9,8},{10,9},{11,10},{13,12},{... | collective-permute-start | bytes 25208 | tf_op jit(solution)/shard_map/ppermute | solution.py:23
  185.1 82.4 %collective-permute-start.27 = (f32[3,4,64]{2,1,0:T(4,128)}, f32[3,4,64]{2,1,0:T(4,128)S(1)}, u32[]{:S(2)}, u32[]{:S(2)}) collective-permute-start(f32[3,4,64]{2,1,0:T(4,128)} %get-tuple-element.392), channel_id=1, source_target_pairs={{0,8},{8,16},{16,24},{1,9},{9,17},{17,25},{2,10},{10,18},{18,26},{... | collective-permute-start | bytes 9224 | tf_op jit(solution)/shard_map/ppermute | solution.py:22
  189.6 78.5 %collective-permute-start.28 = (f32[3,4,64]{2,1,0:T(4,128)}, f32[3,4,64]{2,1,0:T(4,128)}, u32[]{:S(2)}, u32[]{:S(2)}) collective-permute-start(f32[3,4,64]{2,1,0:T(4,128)} %get-tuple-element.393), channel_id=1, source_target_pairs={{8,0},{16,8},{24,16},{9,1},{17,9},{25,17},{10,2},{18,10},{26,18},{... | collective-permute-start | bytes 9224 | tf_op jit(solution)/shard_map/ppermute | solution.py:23
  672.0 17.5 %collective-permute-start.96 = (f32[1,8,128]{2,1,0:T(8,128)S(1)}, f32[1,8,128]{2,1,0:T(8,128)S(1)}, u32[]{:S(2)}, u32[]{:S(2)}) collective-permute-start(f32[1,8,128]{2,1,0:T(8,128)S(1)} %get-tuple-element.330), channel_id=1, source_target_pairs={{0,8},{8,16},{16,24},{1,9},{9,17},{17,25},{2,10},{10,18},{18,26},{... | collective-permute-start | bytes 12296 | tf_op jit(solution)/shard_map/ppermute | solution.py:22
  676.2 13.3 %collective-permute-start.97 = (f32[1,8,128]{2,1,0:T(8,128)S(1)}, f32[1,8,128]{2,1,0:T(8,128)S(1)}, u32[]{:S(2)}, u32[]{:S(2)}) collective-permute-start(f32[1,8,128]{2,1,0:T(8,128)S(1)} %get-tuple-element.331), channel_id=1, source_target_pairs={{8,0},{16,8},{24,16},{9,1},{17,9},{25,17},{10,2},{18,10},{26,18},{... | collective-permute-start | bytes 12296 | tf_op jit(solution)/shard_map/ppermute | solution.py:23
  677.5 14.7 %collective-permute-start.93 = (f32[1,8,128]{2,1,0:T(8,128)S(1)}, f32[1,8,128]{2,1,0:T(8,128)S(1)}, u32[]{:S(2)}, u32[]{:S(2)}) collective-permute-start(f32[1,8,128]{2,1,0:T(8,128)S(1)} %get-tuple-element.328), channel_id=1, source_target_pairs={{0,8},{8,16},{16,24},{1,9},{9,17},{17,25},{2,10},{10,18},{18,26},{... | collective-permute-start | bytes 12296 | tf_op jit(solution)/shard_map/ppermute | solution.py:22
  682.8 9.4 collective-permute-start.94
  684.1 13.5 %collective-permute-start.92 = (f32[1,8,128]{2,1,0:T(8,128)S(1)}, f32[1,8,128]{2,1,0:T(8,128)S(1)}, u32[]{:S(2)}, u32[]{:S(2)}) collective-permute-start(f32[1,8,128]{2,1,0:T(8,128)S(1)} %slice.3788), channel_id=1, source_target_pairs={{0,8},{8,16},{16,24},{1,9},{9,17},{17,25},{2,10},{10,18},{18,26},{... | collective-permute-start | bytes 12296 | tf_op jit(solution)/shard_map/ppermute | solution.py:22
  (249 other events, 3066.5 us)
where the time goes:
time: 1210 us; the launch traced here: 1200 us
  blocking collectives  366 us (30%)
  starting transfers between devices  362 us (30%)
  waiting for transfers between devices  199 us (16%)
  local copies, waits for them, and re-layouts  116 us (10%)
  other arithmetic  98.5 us (8%)
  loops' own time  30.7 us (3%)
  matrix products  15.9 us (1%)
    all_gather x5, blocking collectives, gather_whole(): gathered = lax.all_gather(flattened, ('gx', 'gy', 'gz'), axis=0, tiled=True)  326 us
    ppermute x82, starting transfers between devices, with_halo(): before = lax.ppermute(last, axis, up)  259 us
    ppermute x78, waiting for transfers between devices, with_halo(): after = lax.ppermute(leading, axis, down)  168 us
    ppermute x78, starting transfers between devices, with_halo(): after = lax.ppermute(leading, axis, down)  102 us
    psum x1, blocking collectives, per_device(): summed = lax.psum((totals[0], totals[1], totals[2]), ('gx', 'gy', 'gz'))  39.7 us
    ppermute x82, waiting for transfers between devices, with_halo(): before = lax.ppermute(last, axis, up)  30.7 us
    add x38, other arithmetic, sweep_inner(): iterate[1:-1, 1:-1, 1:-1]  28.9 us
  transfers between devices with their start and end apart: 160, of which 82 were waited for; matrix products, arithmetic and copies ran while one was open for 5% of the time, Pallas kernels for 0%

commit v1 on v0

--- a/solution.py
+++ b/solution.py
@@ -1,6 +1,10 @@
+import functools
+
 import jax
 import jax.numpy as jnp
 from jax import lax
+from jax.experimental import pallas as pl
+from jax.experimental.pallas import tpu as pltpu
 from jax.sharding import PartitionSpec as P
 
 SWEEPS = 3
@@ -411,6 +415,467 @@
     return (new_velocity, summed[0], summed[1], summed[2])
 
 
+F32 = jnp.float32
+BF16 = jnp.bfloat16
+MSG = 11
+VMEM_BYTES = 56 * 1024 * 1024
+
+
+def iota(shape, dim):
+    return lax.broadcasted_iota(jnp.int32, shape, dim)
+
+
+def ahead(plane, step, dim):
+    return pltpu.roll(plane, plane.shape[dim] - step, dim)
+
+
+def behind(plane, step, dim):
+    return pltpu.roll(plane, step, dim)
+
+
+def write_message(msg_ref, fields, sign):
+    first, second, third = fields
+    span, rows, lanes = first.shape
+    row = iota((rows, lanes), 0)
+    lane = iota((rows, lanes), 1)
+    second_face = jnp.zeros((rows, lanes), F32)
+    third_face = jnp.zeros((rows, lanes), F32)
+    for x in range(span):
+        total = first[x] + second[x] + third[x]
+        if x > 0:
+            total = total - first[x - 1]
+        total = total - jnp.where(row == 0, 0.0, behind(second[x], 1, 0))
+        total = total - jnp.where(lane == 0, 0.0, behind(third[x], 1, 1))
+        msg_ref[x] = sign * total
+        second_face = jnp.where(row == x, behind(second[x], x + 1, 0) if x < rows - 1 else second[x], second_face)
+        third_face = jnp.where(lane == x, behind(third[x], x + 1, 1), third_face)
+    msg_ref[span] = -sign * first[span - 1]
+    msg_ref[span + 1] = -sign * second_face
+    msg_ref[span + 2] = -sign * third_face
+
+
+def local_outlets(open_ref, counts, shape):
+    span, rows, lanes = shape
+    here = [lax.axis_index(name) == count - 1 for name, count in zip(("gx", "gy", "gz"), counts)]
+    one = jnp.float32(1.0)
+    ends = [jnp.where(here[d], open_ref[2 * d + 1], one) for d in range(3)]
+    row = iota((rows, lanes), 0)
+    lane = iota((rows, lanes), 1)
+    second = jnp.where(row == rows - 1, ends[1], one)
+    third = jnp.where(lane == lanes - 1, ends[2], one)
+    return ends[0], second, third
+
+
+def forward_kernel(counts, open_ref, cols_ref, vel_ref, win_ref, bias_ref, wout_ref, flux_ref, msg_ref, corr):
+    _, span, rows, lanes = vel_ref.shape
+    chunk = rows * lanes
+    for x in range(span):
+        before = jnp.dot(win_ref[...], cols_ref[:, x * chunk : (x + 1) * chunk], preferred_element_type=F32)
+        before = before + bias_ref[...]
+        hidden = (before * jax.nn.sigmoid(before)).astype(BF16)
+        out = jnp.dot(wout_ref[...], hidden, preferred_element_type=F32)
+        for d in range(3):
+            for y in range(rows):
+                corr[d, x, y : y + 1, :] = out[d : d + 1, y * lanes : (y + 1) * lanes]
+    first_end, second, third = local_outlets(open_ref, counts, (span, rows, lanes))
+    fields = []
+    for d in range(3):
+        planes = []
+        for x in range(span):
+            plane = vel_ref[d, x] + corr[d, x]
+            if d == 0:
+                plane = plane * first_end if x == span - 1 else plane
+            else:
+                plane = plane * (second if d == 1 else third)
+            flux_ref[d, x] = plane
+            planes.append(plane)
+        fields.append(jnp.stack(planes))
+    write_message(msg_ref, fields, -1.0)
+
+
+class Level:
+    pass
+
+
+def pair_sum(plane, step):
+    rows, lanes = plane.shape
+    row = iota((rows, lanes), 0)
+    lane = iota((rows, lanes), 1)
+    odd = lax.rem(row // step, 2) == 1
+    plane = plane + jnp.where(odd, behind(plane, step, 0), ahead(plane, step, 0))
+    odd = lax.rem(lane // step, 2) == 1
+    return plane + jnp.where(odd, behind(plane, step, 1), ahead(plane, step, 1))
+
+
+def raw_upper(level, open_ref, x):
+    rows, lanes = level.rho.shape[1:]
+    row = iota((rows, lanes), 0)
+    lane = iota((rows, lanes), 1)
+    step = level.step
+    rho = level.rho[x + 1]
+    last_row = row >= rows - step
+    last_lane = lane >= lanes - step
+    one = jnp.float32(1.0)
+    up0 = jnp.where(x == level.span - 1, open_ref[1], one) * (2.0 * level.weight) / (rho + level.rho[x + 2])
+    up1 = (2.0 * level.weight) / (rho + jnp.where(last_row, 0.0, ahead(rho, step, 0)))
+    up1 = up1 * jnp.where(last_row, open_ref[3], one)
+    up2 = (2.0 * level.weight) / (rho + jnp.where(last_lane, 0.0, ahead(rho, step, 1)))
+    up2 = up2 * jnp.where(last_lane, open_ref[5], one)
+    return up0, up1, up2
+
+
+def build_level(level, open_ref):
+    rows, lanes = level.rho.shape[1:]
+    step = level.step
+
+    def body(x, unused):
+        row = iota((rows, lanes), 0)
+        lane = iota((rows, lanes), 1)
+        one = jnp.float32(1.0)
+        rho = level.rho[x + 1]
+        up0, up1, up2 = raw_upper(level, open_ref, x)
+        twice = 2.0 * level.weight
+        down0 = jnp.where(x == 0, open_ref[0], one) * twice / (rho + level.rho[x])
+        first_row = row < step
+        first_lane = lane < step
+        down1 = jnp.where(first_row, open_ref[2] * twice / rho, behind(up1, step, 0))
+        down2 = jnp.where(first_lane, open_ref[4] * twice / rho, behind(up2, step, 1))
+        diagonal = MASS_SHIFT + up0 + down0 + up1 + down1 + up2 + down2
+        scale = RELAXATION / diagonal
+        level.scale[x] = scale
+        level.unscale[x] = diagonal * (1.0 / RELAXATION)
+        level.coef[0, x] = scale * up0
+        level.coef[1, x] = scale * down0
+        level.coef[2, x] = jnp.where(row >= rows - step, 0.0, scale * up1)
+        level.coef[3, x] = jnp.where(first_row, 0.0, scale * down1)
+        level.coef[4, x] = jnp.where(lane >= lanes - step, 0.0, scale * up2)
+        level.coef[5, x] = jnp.where(first_lane, 0.0, scale * down2)
+        return unused
+
+    lax.fori_loop(0, level.span, body, 0)
+
+
+def smoothed(level, src, scaled, x):
+    step = level.step
+    mid = src[x + 1]
+    total = scaled[x + 1] + (1.0 - RELAXATION) * mid
+    total = total + (level.coef[0, x] * src[x + 2] + level.coef[1, x] * src[x])
+    total = total + (level.coef[2, x] * ahead(mid, step, 0) + level.coef[3, x] * behind(mid, step, 0))
+    return total + (level.coef[4, x] * ahead(mid, step, 1) + level.coef[5, x] * behind(mid, step, 1))
+
+
+def loop(count, body):
+    def step(x, unused):
+        body(x)
+        return unused
+
+    lax.fori_loop(0, count, step, 0, unroll=2)
+
+
+def sweep(level, src, dst, scaled):
+    def body(x):
+        dst[x + 1] = smoothed(level, src, scaled, x)
+
+    loop(level.span, body)
+
+
+def cycle(levels, scaled, one, two):
+    level = levels[0]
+    if len(levels) == 1:
+        src, dst, spare = scaled, one, two
+        for repeat in range(COARSE_SWEEPS - 1):
+            sweep(level, src, dst, scaled)
+            src, dst, spare = dst, spare, dst
+        return src
+    sweep(level, scaled, one, scaled)
+    src, dst = one, two
+    for repeat in range(SWEEPS - 2):
+        sweep(level, src, dst, scaled)
+        src, dst = dst, src
+    below = levels[1]
+
+    def lower(x):
+        even = (smoothed(level, src, scaled, 2 * x) - src[2 * x + 1]) * level.unscale[2 * x]
+        odd = (smoothed(level, src, scaled, 2 * x + 1) - src[2 * x + 2]) * level.unscale[2 * x + 1]
+        below.scaled[x + 1] = pair_sum(even + odd, level.step) * 0.125 * below.scale[x]
+
+    lax.fori_loop(0, below.span, lambda x, unused: (lower(x), unused)[1], 0)
+    coarse = cycle(levels[1:], below.scaled, below.one, below.two)
+
+    def raise_(x):
+        extra = coarse[x + 1]
+        src[2 * x + 1] = src[2 * x + 1] + extra
+        src[2 * x + 2] = src[2 * x + 2] + extra
+
+    loop(below.span, raise_)
+    for repeat in range(SWEEPS):
+        sweep(level, src, dst, scaled)
+        src, dst = dst, src
+    return src
+
+
+def make_levels(refs):
+    levels = []
+    for depth in range(3):
+        level = Level()
+        level.step = 2**depth
+        level.weight = 0.25**depth
+        level.rho, level.scale, level.unscale, level.coef, level.scaled, level.one, level.two = refs[7 * depth : 7 * depth + 7]
+        level.span = level.scale.shape[0]
+        levels.append(level)
+    return levels
+
+
+def level_scratch(whole):
+    shapes = []
+    for depth in range(3):
+        span = whole[0] // 2**depth
+        plane = tuple(whole[1:])
+        padded = pltpu.VMEM((span + 2,) + plane, F32)
+        flat = pltpu.VMEM((span,) + plane, F32)
+        shapes += [padded, flat, flat, pltpu.VMEM((6, span) + plane, F32), padded, padded, padded]
+    return shapes
+
+
+def clear_ends(ref):
+    zero = jnp.zeros(ref.shape[1:], F32)
+    ref[0] = zero
+    ref[ref.shape[0] - 1] = zero
+
+
+def prepare(levels, open_ref, density_ref, counts):
+    blocks, span, rows, lanes = density_ref.shape
+    for level in levels:
+        for ref in (level.rho, level.scaled, level.one, level.two):
+            clear_ends(ref)
+    for i in range(counts[0]):
+        for j in range(counts[1]):
+            for k in range(counts[2]):
+                block = (i * counts[1] + j) * counts[2] + k
+                levels[0].rho[
+                    1 + span * i : 1 + span * (i + 1), rows * j : rows * (j + 1), lanes * k : lanes * (k + 1)
+                ] = density_ref[block]
+    for level, below in zip(levels[:-1], levels[1:]):
+
+        def body(x, level=level, below=below):
+            below.rho[x + 1] = pair_sum(level.rho[2 * x + 1] + level.rho[2 * x + 2], level.step) * 0.125
+
+        loop(below.span, body)
+    for level in levels:
+        build_level(level, open_ref)
+
+
+def assemble(target, msg_ref, counts):
+    blocks, planes, rows, lanes = msg_ref.shape
+    span = planes - 3
+    lane = iota((rows, lanes), 1)
+    for i in range(counts[0]):
+        for j in range(counts[1]):
+            for k in range(counts[2]):
+                block = (i * counts[1] + j) * counts[2] + k
+                at_rows = slice(rows * j, rows * (j + 1))
+                at_lanes = slice(lanes * k, lanes * (k + 1))
+                for x in range(span):
+                    plane = msg_ref[block, x]
+                    if x == 0 and i > 0:
+                        plane = plane + msg_ref[block - counts[1] * counts[2], span]
+                    if k > 0:
+                        face = msg_ref[block - 1, span + 2]
+                        face = ahead(face, x, 1) if x > 0 else face
+                        plane = plane + jnp.where(lane == 0, face, 0.0)
+                    target[1 + span * i + x, at_rows, at_lanes] = plane
+                    if j > 0:
+                        face = msg_ref[block - counts[2], span + 1, x : x + 1, :]
+                        at_row = slice(rows * j, rows * j + 1)
+                        target[1 + span * i + x, at_row, at_lanes] = (
+                            target[1 + span * i + x, at_row, at_lanes] + face
+                        )
+
+
+def solve(levels, msg_ref, counts, kept):
+    fine = levels[0]
+    assemble(fine.scaled, msg_ref, counts)
+
+    def scale(x):
+        fine.scaled[x + 1] = fine.scaled[x + 1] * fine.scale[x]
+
+    loop(fine.span, scale)
+    first = cycle(levels, fine.scaled, fine.one, fine.two)
+
+    def again(x):
+        mid = first[x + 1]
+        kept[x + 1] = mid
+        fine.again[x + 1] = smoothed(fine, first, fine.scaled, x) - mid
+
+    loop(fine.span, again)
+    second = cycle(levels, fine.again, fine.one, fine.two)
+
+    def add(x):
+        kept[x + 1] = kept[x + 1] + second[x + 1]
+
+    loop(fine.span, add)
+
+
+def rises(kept, wide, slot, start, span):
+    rows, lanes = kept.shape[1:]
+
+    def body(x, unused):
+        row = iota((rows, lanes), 0)
+        lane = iota((rows, lanes), 1)
+        mid = kept[start + x + 1]
+        wide[slot, x] = kept[start + x + 2] - mid
+        wide[slot + 1, x] = jnp.where(row == rows - 1, 0.0, ahead(mid, 1, 0)) - mid
+        wide[slot + 2, x] = jnp.where(lane == lanes - 1, 0.0, ahead(mid, 1, 1)) - mid
+        return unused
+
+    lax.fori_loop(0, span, body, 0)
+
+
+def own_block(wide, slot, rows, lanes):
+    j = lax.axis_index("gy")
+    k = lax.axis_index("gz")
+    return wide[slot, :, pl.ds(pl.multiple_of(j * rows, rows), rows), pl.ds(pl.multiple_of(k * lanes, lanes), lanes)]
+
+
+def project_kernel(counts, open_ref, density_ref, msg_ref, flux_ref, target_ref, new_ref, misfit_ref, out_ref, kept, extra, wide, *refs):
+    levels = make_levels(refs)
+    fine = levels[0]
+    fine.again = extra
+    clear_ends(kept)
+    clear_ends(extra)
+    prepare(levels, open_ref, density_ref, counts)
+    solve(levels, msg_ref, counts, kept)
+    _, span, rows, lanes = flux_ref.shape
+    start = lax.axis_index("gx") * span
+    rises(kept, wide, 0, start, span)
+
+    def body(x, unused):
+        ups = raw_upper(fine, open_ref, start + x)
+        for d in range(3):
+            wide[3 + d, x] = ups[d]
+        return unused
+
+    lax.fori_loop(0, span, body, 0)
+    cells = counts[0] * counts[1] * counts[2] * span * rows * lanes
+    fields = []
+    for d in range(3):
+        upper = own_block(wide, 3 + d, rows, lanes)
+        fresh = flux_ref[d] - upper * own_block(wide, d, rows, lanes)
+        new_ref[d] = fresh
+        misfit = (fresh - target_ref[d]) / cells
+        misfit_ref[d] = misfit
+        fields.append(upper * misfit)
+    write_message(out_ref, fields, 1.0)
+
+
+def adjoint_kernel(counts, open_ref, density_ref, msg_ref, misfit_ref, cols_ref, win_ref, bias_ref, wout_ref, out_ref, upstream, kept, extra, wide, *refs):
+    levels = make_levels(refs)
+    fine = levels[0]
+    fine.again = extra
+    clear_ends(kept)
+    clear_ends(extra)
+    prepare(levels, open_ref, density_ref, counts)
+    solve(levels, msg_ref, counts, kept)
+    _, span, rows, lanes = misfit_ref.shape
+    start = lax.axis_index("gx") * span
+    rises(kept, wide, 0, start, span)
+    first_end, second, third = local_outlets(open_ref, counts, (span, rows, lanes))
+    chunk = rows * lanes
+    upstream[...] = jnp.zeros(upstream.shape, F32)
+    for d in range(3):
+        block = misfit_ref[d] + own_block(wide, d, rows, lanes)
+        for x in range(span):
+            plane = block[x]
+            if d == 0:
+                plane = plane * first_end if x == span - 1 else plane
+            else:
+                plane = plane * (second if d == 1 else third)
+            for y in range(rows):
+                upstream[d : d + 1, x * chunk + y * lanes : x * chunk + (y + 1) * lanes] = plane[y : y + 1]
+    across = (((1,), (1,)), ((), ()))
+    hidden_size = win_ref.shape[0]
+    feat = win_ref.shape[1]
+    grad_in = jnp.zeros((feat, hidden_size), F32)
+    grad_out = jnp.zeros((8, hidden_size), F32)
+    grad_bias = jnp.zeros((8, hidden_size), F32)
+    ones = jnp.ones((8, chunk), BF16)
+    for x in range(span):
+        columns = cols_ref[:, x * chunk : (x + 1) * chunk]
+        before = jnp.dot(win_ref[...], columns, preferred_element_type=F32) + bias_ref[...]
+        gate = jax.nn.sigmoid(before)
+        hidden = (before * gate).astype(BF16)
+        up = upstream[:, x * chunk : (x + 1) * chunk].astype(BF16)
+        grad_out = grad_out + lax.dot_general(up, hidden, across, preferred_element_type=F32)
+        grad_hidden = lax.dot_general(wout_ref[...], up, (((0,), (0,)), ((), ())), preferred_element_type=F32)
+        grad_before = grad_hidden * (gate * (1.0 + before * (1.0 - gate)))
+        high = grad_before.astype(BF16)
+        low = (grad_before - high.astype(F32)).astype(BF16)
+        grad_bias = grad_bias + lax.dot_general(ones, high, across, preferred_element_type=F32)
+        grad_bias = grad_bias + lax.dot_general(ones, low, across, preferred_element_type=F32)
+        grad_in = grad_in + lax.dot_general(columns, high, across, preferred_element_type=F32)
+    out_ref[0:feat, :] = grad_in
+    out_ref[feat : feat + 8, :] = grad_out
+    out_ref[feat + 8 : feat + 16, :] = grad_bias
+
+
+def whole_device(counts, velocity, features, density, target, weight_in, bias_in, weight_out, open_faces):
+    axes = ("gx", "gy", "gz")
+    shape = density.shape
+    span, rows, lanes = shape
+    whole = tuple(n * c for n, c in zip(shape, counts))
+    feat, hidden_size = weight_in.shape
+    cells = span * rows * lanes
+    opens = open_faces.astype(F32)
+    columns = features.reshape(feat, cells)
+    win = weight_in.T
+    bias = bias_in.reshape(hidden_size, 1)
+    wout = jnp.pad(weight_out.T, ((0, 5), (0, 0)))
+    vmem = pl.BlockSpec(memory_space=pltpu.VMEM)
+    smem = pl.BlockSpec(memory_space=pltpu.SMEM)
+    params = pltpu.CompilerParams(vmem_limit_bytes=VMEM_BYTES)
+    blocks = lax.all_gather(density, axes, axis=0)
+    field = jax.ShapeDtypeStruct((3,) + shape, F32)
+    message = jax.ShapeDtypeStruct((span + 3, rows, lanes), F32)
+    flux, msg = pl.pallas_call(
+        functools.partial(forward_kernel, counts),
+        out_shape=(field, message),
+        in_specs=[smem] + [vmem] * 5,
+        out_specs=(vmem, vmem),
+        scratch_shapes=[pltpu.VMEM((3,) + shape, F32)],
+        compiler_params=params,
+        name="closure_forward",
+    )(opens, columns, velocity, win, bias, wout)
+    sources = lax.all_gather(msg, axes, axis=0)
+    padded = pltpu.VMEM((whole[0] + 2,) + whole[1:], F32)
+    wide = pltpu.VMEM((6, span) + whole[1:], F32)
+    scratch = [padded, padded, wide] + level_scratch(whole)
+    new_velocity, misfit, msg = pl.pallas_call(
+        functools.partial(project_kernel, counts),
+        out_shape=(field, field, message),
+        in_specs=[smem] + [vmem] * 4,
+        out_specs=(vmem, vmem, vmem),
+        scratch_shapes=scratch,
+        compiler_params=params,
+        name="project",
+    )(opens, blocks, sources, flux, target)
+    sources = lax.all_gather(msg, axes, axis=0)
+    sums = pl.pallas_call(
+        functools.partial(adjoint_kernel, counts),
+        out_shape=jax.ShapeDtypeStruct((feat + 16, hidden_size), F32),
+        in_specs=[smem] + [vmem] * 7,
+        out_specs=vmem,
+        scratch_shapes=[pltpu.VMEM((8, cells), F32)] + scratch,
+        compiler_params=params,
+        name="adjoint",
+    )(opens, blocks, sources, misfit, columns, win, bias, wout)
+    sums = lax.psum(sums, axes)
+    return new_velocity, sums[:feat], sums[feat + 8], sums[feat : feat + 3].T
+
+
+def fits(mesh):
+    return mesh.size <= 32
+
+
 def solution(mesh):
     in_specs = (
         P(None, "gx", "gy", "gz"),
@@ -423,6 +888,8 @@
         P(),
     )
     out_specs = (P(None, "gx", "gy", "gz"), P(), P(), P())
+    counts = tuple(mesh.shape[name] for name in ("gx", "gy", "gz"))
+    body = functools.partial(whole_device, counts) if fits(mesh) else per_device
     return jax.shard_map(
-        per_device, mesh=mesh, in_specs=in_specs, out_specs=out_specs, check_vma=False
-    )
+        body, mesh=mesh, in_specs=in_specs, out_specs=out_specs, check_vma=False
+    )

time: 1210 us -> 344 us (0.28); the launches traced: 1200 us -> 343 us
  starting transfers between devices: 362 us -> 0.12 us
  blocking collectives: 366 us -> 39.2 us
  Pallas kernels: 0 us -> 121 us
  local copies, waits for them, and re-layouts: 116 us -> 7.5 us
  other arithmetic: 98.5 us -> 1.17 us
  waiting for transfers between devices: 199 us -> 161 us
  loops' own time: 30.7 us -> 0 us
  matrix products: 15.9 us -> 0 us
    ppermute x160 -> x0, starting transfers between devices: 362 us -> none  [the longest x82 259 us: with_halo(): before = lax.ppermute(last, axis, up)]
    all_gather x5 -> x0, blocking collectives: 326 us -> none  [gather_whole(): gathered = lax.all_gather(flattened, ('gx', 'gy', 'gz'), axis=0, tiled=True)]
    ppermute x160 -> x0, waiting for transfers between devices: 199 us -> none  [the longest x78 168 us: with_halo(): after = lax.ppermute(leading, axis, down)]
    all_gather x0 -> x3, waiting for transfers between devices: none -> 160 us  [the longest x2 111 us: whole_device(): sources = lax.all_gather(msg, axes, axis=0)]
    pallas_call x0 -> x3, Pallas kernels: none -> 121 us  [the longest x1 59.6 us: whole_device(): pl.pallas_call(functools.partial(adjoint_kernel, counts), out_shape=jax.S...]
    reshape x32 -> x1, local copies, waits for them, and re-layouts: 56.1 us -> 1.34 us  [whole_device(): bias = bias_in.reshape(hidden_size, 1)]
    add x81 -> x0, other arithmetic: 48 us -> none  [the longest x38 28.9 us: sweep_inner(): iterate[1:-1, 1:-1, 1:-1]]
    another operation x2 -> x0, loops' own time: 30.7 us -> none  [the longest x1 15.8 us: closure_gradients(): lax.scan(step_plane, start, jnp.arange(features.shape[1], dtype=jnp.int32))]
  transfers between devices with their start and end apart: 160 -> 3, of which waited for: 82 -> 3; matrix products, arithmetic and copies ran while one was open for 5% -> 2% of each run, Pallas kernels for 0% -> 1%
where the time goes in v1:
time: 344 us; the launch traced here: 343 us
  waiting for transfers between devices  161 us (47%)
  Pallas kernels  121 us (35%)
  blocking collectives  39.2 us (11%)
  between operations  13.7 us (4%)
  local copies, waits for them, and re-layouts  7.5 us (2%)
    all_gather x2, waiting for transfers between devices, whole_device(): sources = lax.all_gather(msg, axes, axis=0)  111 us
    pallas_call x1, Pallas kernels, whole_device(): pl.pallas_call(functools.partial(adjoint_kernel, counts), out_shape=jax.S...  59.6 us
    pallas_call x1, Pallas kernels, whole_device(): pl.pallas_call(functools.partial(project_kernel, counts), out_shape=(fiel...  57.8 us
    all_gather x1, waiting for transfers between devices, whole_device(): blocks = lax.all_gather(density, axes, axis=0)  49.2 us
    psum x1, blocking collectives, whole_device(): sums = lax.psum(sums, axes)  39.2 us
  transfers between devices with their start and end apart: 3, of which 3 were waited for; matrix products, arithmetic and copies ran while one was open for 2% of the time, Pallas kernels for 1%

profile of v1, /device:TPU:0, one launch (start us, length us, event | category | flops | bytes accessed | tf_op | source)
XLA Modules:
  0.0 343.4 jit_solution(11980912705680037101)
XLA Ops:
  7.2 0.0 all-gather.7.cloned.1.call-start
  7.2 0.7 all-gather.7.cloned.1.call-update
  7.9 0.0 all-gather.9.cloned.1.call-start
  7.9 1.2 convert_element_type.5.open_ref
  9.1 1.4 copy.15
  10.5 1.3 copy.16.bias_ref
  11.8 1.8 copy.20
  13.7 1.3 pad.4.wout_ref
  14.9 3.3 closure_forward.1
  18.2 0.0 all-gather.9.cloned.1.call-update
  18.2 0.0 all-gather.11.cloned.1.call-start
  18.3 49.2 %all-gather.7.cloned.1.call-done = f32[256,8,128]{2,1,0:T(8,128)} async-done(((f32[8,8,128]{2,1,0:T(8,128)}), f32[256,8,128]{2,1,0:T(8,128)}) %all-gather.7.cloned.1.call-update) | async-done | bytes 1048592 | tf_op jit(solution)/shard_map/all_gather | solution.py:836
  67.5 57.2 %all-gather.9.cloned.1.call-done = f32[352,8,128]{2,1,0:T(8,128)} async-done(((f32[11,8,128]{2,1,0:T(8,128)}), f32[352,8,128]{2,1,0:T(8,128)}) %all-gather.9.cloned.1.call-update) | async-done | bytes 1441808 | tf_op jit(solution)/shard_map/all_gather | solution.py:848
  124.7 57.8 %project.1 = (f32[3,8,8,128]{3,2,1,0:T(8,128)}, f32[3,8,8,128]{3,2,1,0:T(8,128)}, f32[11,8,128]{2,1,0:T(8,128)}) custom-call(f32[6]{0:T(128)} %convert_element_type.5.open_ref, f32[32,8,8,128]{3,2,1,0:T(8,128)} %bitcast.15, f32[32,11,8,128]{3,2,1,0:T(8,128)} %bitcast.19, f32[3,8,8,128]{3,2,1,0:T(8,128)} %get-tuple-element.10.flux_ref, ...), custom_call_target="tpu_custom_call" | custom-call | tf_op jit(solution)/shard_map/project/pallas_call | solution.py:852
  182.4 0.0 all-gather.11.cloned.1.call-update
  182.4 53.9 %all-gather.11.cloned.1.call-done = f32[352,8,128]{2,1,0:T(8,128)} async-done(((f32[11,8,128]{2,1,0:T(8,128)}), f32[352,8,128]{2,1,0:T(8,128)}) %all-gather.11.cloned.1.call-update) | async-done | bytes 1441808 | tf_op jit(solution)/shard_map/all_gather | solution.py:861
  236.4 59.6 %adjoint.1 = f32[32,64]{1,0:T(8,128)} custom-call(f32[6]{0:T(128)} %convert_element_type.5.open_ref, f32[32,8,8,128]{3,2,1,0:T(8,128)} %bitcast.16, f32[32,11,8,128]{3,2,1,0:T(8,128)} %bitcast.20, f32[3,8,8,128]{3,2,1,0:T(8,128)} %get-tuple-element.13.misfit_ref, bf16[16,8192]{1,0:T(8,128)(2,1)} %bitcast.18, bf16[64,16]{1,0:T(8,128)(2,1)} %bitcast.23, ...), custom_call_target="tpu_custom_call" | custom-call | tf_op jit(solution)/shard_map/adjoint/pallas_call | solution.py:862
  296.0 39.2 %psum.7 = f32[32,64]{1,0:T(8,128)S(1)} all-reduce(f32[32,64]{1,0:T(8,128)} %adjoint.1), channel_id=1, replica_groups=mesh['gx'=4,'gy'=2,'gz'=4] {'gx','gy','gz'}, use_global_device_ids=true, to_apply=%region_0.1 | all-reduce | flops 2048 | bytes 16384 | tf_op jit(solution)/shard_map/psum | solution.py:871
  335.1 0.5 slice_bitcast_fusion.1
  335.6 0.6 slice_bitcast_fusion
  336.2 0.6 slice.12
Async XLA Ops:
  7.2 60.3 %all-gather.7.cloned.1.call-start = ((), (), s32[]{:S(2)}) async-start(), calls=%async_computation | async-start | bytes 1081344 | tf_op jit(solution)/shard_map/all_gather | solution.py:836
  7.9 116.8 %all-gather.9.cloned.1.call-start = ((), (), s32[]{:S(2)}) async-start(), calls=%async_computation.1 | async-start | bytes 1486848 | tf_op jit(solution)/shard_map/all_gather | solution.py:848
  18.2 218.2 %all-gather.11.cloned.1.call-start = ((), (), s32[]{:S(2)}) async-start(), calls=%async_computation.2 | async-start | bytes 1486848 | tf_op jit(solution)/shard_map/all_gather | solution.py:861
Sparse Core Ops, SparseCore 0:
  11.0 56.4 all-gather.6
  70.9 53.7 all-gather.8
  182.6 53.7 all-gather.10

commit v2 on v1

--- a/solution.py
+++ b/solution.py
@@ -418,7 +418,14 @@
 F32 = jnp.float32
 BF16 = jnp.bfloat16
 MSG = 11
+DOWN = (((0,), (0,)), ((), ()))
+AXES = ("gx", "gy", "gz")
+TILE = 128
 VMEM_BYTES = 56 * 1024 * 1024
+
+
+def opened(open_ref, face):
+    return open_ref[face].astype(F32)
 
 
 def iota(shape, dim):
@@ -458,7 +465,7 @@
     span, rows, lanes = shape
     here = [lax.axis_index(name) == count - 1 for name, count in zip(("gx", "gy", "gz"), counts)]
     one = jnp.float32(1.0)
-    ends = [jnp.where(here[d], open_ref[2 * d + 1], one) for d in range(3)]
+    ends = [jnp.where(here[d], opened(open_ref, 2 * d + 1), one) for d in range(3)]
     row = iota((rows, lanes), 0)
     lane = iota((rows, lanes), 1)
     second = jnp.where(row == rows - 1, ends[1], one)
@@ -470,10 +477,10 @@
     _, span, rows, lanes = vel_ref.shape
     chunk = rows * lanes
     for x in range(span):
-        before = jnp.dot(win_ref[...], cols_ref[:, x * chunk : (x + 1) * chunk], preferred_element_type=F32)
+        before = lax.dot_general(win_ref[...], cols_ref[:, x * chunk : (x + 1) * chunk], DOWN, preferred_element_type=F32)
         before = before + bias_ref[...]
         hidden = (before * jax.nn.sigmoid(before)).astype(BF16)
-        out = jnp.dot(wout_ref[...], hidden, preferred_element_type=F32)
+        out = lax.dot_general(wout_ref[...], hidden, DOWN, preferred_element_type=F32)
         for d in range(3):
             for y in range(rows):
                 corr[d, x, y : y + 1, :] = out[d : d + 1, y * lanes : (y + 1) * lanes]
@@ -497,6 +504,63 @@
     pass
 
 
+def exact_dot(values, ones):
+    high = values.astype(BF16)
+    low = (values - high.astype(F32)).astype(BF16)
+    total = jnp.dot(high, ones, preferred_element_type=F32)
+    return total + jnp.dot(low, ones, preferred_element_type=F32)
+
+
+def pair_matrices(tools):
+    gather, spread = tools[0], tools[1]
+    for ref, fine, coarse in ((gather, 0, 1), (spread, 1, 0)):
+        hit = iota(ref.shape, fine) // 2 == iota(ref.shape, coarse)
+        ref[...] = jnp.where(hit, 1.0, 0.0).astype(BF16)
+
+
+def block_means(tools, span, plane_of, put):
+    gather, _, narrow, small, tall, _ = tools
+    half = tall.shape[2] // 2
+
+    def fold(x):
+        plane = plane_of(x)
+        for tile in range(tall.shape[1]):
+            at = slice(tile * TILE, (tile + 1) * TILE)
+            tall[x, tile] = plane[:, at]
+            even = tall[x, tile, pl.ds(0, half, stride=2), :]
+            odd = tall[x, tile, pl.ds(1, half, stride=2), :]
+            narrow[pl.ds(pl.multiple_of(x * half, half), half), at] = even + odd
+
+    loop(span, fold)
+    small[...] = exact_dot(narrow[...], gather[...]) * 0.125
+
+    def finish(x):
+        put(x, small[pl.ds(pl.multiple_of(x * half, half), half), :])
+
+    loop(span, finish)
+
+
+def copy_to_fine(tools, span, coarse, put):
+    _, spread, narrow, small, _, tall = tools
+    half = tall.shape[2] // 2
+
+    def pick(x):
+        small[pl.ds(pl.multiple_of(x * half, half), half), :] = coarse[x + 1]
+
+    loop(span, pick)
+    narrow[...] = exact_dot(small[...], spread[...])
+
+    def finish(x):
+        rows = narrow[pl.ds(pl.multiple_of(x * half, half), half), :]
+        for tile in range(tall.shape[1]):
+            part = rows[:, tile * TILE : (tile + 1) * TILE]
+            tall[x, tile, pl.ds(0, half, stride=2), :] = part
+            tall[x, tile, pl.ds(1, half, stride=2), :] = part
+        put(x, jnp.concatenate([tall[x, tile] for tile in range(tall.shape[1])], axis=1))
+
+    loop(span, finish)
+
+
 def pair_sum(plane, step):
     rows, lanes = plane.shape
     row = iota((rows, lanes), 0)
@@ -516,11 +580,11 @@
     last_row = row >= rows - step
     last_lane = lane >= lanes - step
     one = jnp.float32(1.0)
-    up0 = jnp.where(x == level.span - 1, open_ref[1], one) * (2.0 * level.weight) / (rho + level.rho[x + 2])
+    up0 = jnp.where(x == level.span - 1, opened(open_ref, 1), one) * (2.0 * level.weight) / (rho + level.rho[x + 2])
     up1 = (2.0 * level.weight) / (rho + jnp.where(last_row, 0.0, ahead(rho, step, 0)))
-    up1 = up1 * jnp.where(last_row, open_ref[3], one)
+    up1 = up1 * jnp.where(last_row, opened(open_ref, 3), one)
     up2 = (2.0 * level.weight) / (rho + jnp.where(last_lane, 0.0, ahead(rho, step, 1)))
-    up2 = up2 * jnp.where(last_lane, open_ref[5], one)
+    up2 = up2 * jnp.where(last_lane, opened(open_ref, 5), one)
     return up0, up1, up2
 
 
@@ -535,11 +599,11 @@
         rho = level.rho[x + 1]
         up0, up1, up2 = raw_upper(level, open_ref, x)
         twice = 2.0 * level.weight
-        down0 = jnp.where(x == 0, open_ref[0], one) * twice / (rho + level.rho[x])
+        down0 = jnp.where(x == 0, opened(open_ref, 0), one) * twice / (rho + level.rho[x])
         first_row = row < step
         first_lane = lane < step
-        down1 = jnp.where(first_row, open_ref[2] * twice / rho, behind(up1, step, 0))
-        down2 = jnp.where(first_lane, open_ref[4] * twice / rho, behind(up2, step, 1))
+        down1 = jnp.where(first_row, opened(open_ref, 2) * twice / rho, behind(up1, step, 0))
+        down2 = jnp.where(first_lane, opened(open_ref, 4) * twice / rho, behind(up2, step, 1))
         diagonal = MASS_SHIFT + up0 + down0 + up1 + down1 + up2 + down2
         scale = RELAXATION / diagonal
         level.scale[x] = scale
@@ -569,7 +633,7 @@
         body(x)
         return unused
 
-    lax.fori_loop(0, count, step, 0, unroll=2)
+    lax.fori_loop(0, count, step, 0, unroll=4)
 
 
 def sweep(level, src, dst, scaled):
@@ -597,17 +661,25 @@
     def lower(x):
         even = (smoothed(level, src, scaled, 2 * x) - src[2 * x + 1]) * level.unscale[2 * x]
         odd = (smoothed(level, src, scaled, 2 * x + 1) - src[2 * x + 2]) * level.unscale[2 * x + 1]
-        below.scaled[x + 1] = pair_sum(even + odd, level.step) * 0.125 * below.scale[x]
-
-    lax.fori_loop(0, below.span, lambda x, unused: (lower(x), unused)[1], 0)
+        return even + odd
+
+    def store(x, mean):
+        below.scaled[x + 1] = mean * below.scale[x]
+
+    if level.tools is not None:
+        block_means(level.tools, below.span, lower, store)
+    else:
+        loop(below.span, lambda x: store(x, pair_sum(lower(x), level.step) * 0.125))
     coarse = cycle(levels[1:], below.scaled, below.one, below.two)
 
-    def raise_(x):
-        extra = coarse[x + 1]
+    def raise_(x, extra):
         src[2 * x + 1] = src[2 * x + 1] + extra
         src[2 * x + 2] = src[2 * x + 2] + extra
 
-    loop(below.span, raise_)
+    if level.tools is not None:
+        copy_to_fine(level.tools, below.span, coarse, raise_)
+    else:
+        loop(below.span, lambda x: raise_(x, coarse[x + 1]))
     for repeat in range(SWEEPS):
         sweep(level, src, dst, scaled)
         src, dst = dst, src
@@ -616,9 +688,12 @@
 
 def make_levels(refs):
     levels = []
+    tools = refs[:6]
+    refs = refs[6:]
     for depth in range(3):
         level = Level()
-        level.step = 2**depth
+        level.step = (1, 1, 2)[depth]
+        level.tools = tools if depth == 0 else None
         level.weight = 0.25**depth
         level.rho, level.scale, level.unscale, level.coef, level.scaled, level.one, level.two = refs[7 * depth : 7 * depth + 7]
         level.span = level.scale.shape[0]
@@ -627,10 +702,18 @@
 
 
 def level_scratch(whole):
-    shapes = []
+    span, rows, lanes = (whole[0] // 2, whole[1] // 2, whole[2] // 2)
+    shapes = [
+        pltpu.VMEM((2 * lanes, lanes), BF16),
+        pltpu.VMEM((lanes, 2 * lanes), BF16),
+        pltpu.VMEM((span * rows, 2 * lanes), F32),
+        pltpu.VMEM((span * rows, lanes), F32),
+        pltpu.VMEM((span, 2 * lanes // TILE, 2 * rows, TILE), F32),
+        pltpu.VMEM((span, 2 * lanes // TILE, 2 * rows, TILE), F32),
+    ]
     for depth in range(3):
         span = whole[0] // 2**depth
-        plane = tuple(whole[1:])
+        plane = tuple(whole[1:]) if depth == 0 else (whole[1] // 2, whole[2] // 2)
         padded = pltpu.VMEM((span + 2,) + plane, F32)
         flat = pltpu.VMEM((span,) + plane, F32)
         shapes += [padded, flat, flat, pltpu.VMEM((6, span) + plane, F32), padded, padded, padded]
@@ -644,48 +727,53 @@
 
 
 def prepare(levels, open_ref, density_ref, counts):
-    blocks, span, rows, lanes = density_ref.shape
+    span, rows, lanes = density_ref.shape[3:]
     for level in levels:
         for ref in (level.rho, level.scaled, level.one, level.two):
             clear_ends(ref)
     for i in range(counts[0]):
         for j in range(counts[1]):
             for k in range(counts[2]):
-                block = (i * counts[1] + j) * counts[2] + k
                 levels[0].rho[
                     1 + span * i : 1 + span * (i + 1), rows * j : rows * (j + 1), lanes * k : lanes * (k + 1)
-                ] = density_ref[block]
+                ] = density_ref[i, k, j]
     for level, below in zip(levels[:-1], levels[1:]):
 
-        def body(x, level=level, below=below):
-            below.rho[x + 1] = pair_sum(level.rho[2 * x + 1] + level.rho[2 * x + 2], level.step) * 0.125
-
-        loop(below.span, body)
+        def total(x, level=level):
+            return level.rho[2 * x + 1] + level.rho[2 * x + 2]
+
+        def store(x, mean, below=below):
+            below.rho[x + 1] = mean
+
+        if level.tools is not None:
+            pair_matrices(level.tools)
+            block_means(level.tools, below.span, total, store)
+        else:
+            loop(below.span, lambda x: store(x, pair_sum(total(x), level.step) * 0.125))
     for level in levels:
         build_level(level, open_ref)
 
 
 def assemble(target, msg_ref, counts):
-    blocks, planes, rows, lanes = msg_ref.shape
+    planes, rows, lanes = msg_ref.shape[3:]
     span = planes - 3
     lane = iota((rows, lanes), 1)
     for i in range(counts[0]):
         for j in range(counts[1]):
             for k in range(counts[2]):
-                block = (i * counts[1] + j) * counts[2] + k
                 at_rows = slice(rows * j, rows * (j + 1))
                 at_lanes = slice(lanes * k, lanes * (k + 1))
                 for x in range(span):
-                    plane = msg_ref[block, x]
+                    plane = msg_ref[i, k, j, x]
                     if x == 0 and i > 0:
-                        plane = plane + msg_ref[block - counts[1] * counts[2], span]
+                        plane = plane + msg_ref[i - 1, k, j, span]
                     if k > 0:
-                        face = msg_ref[block - 1, span + 2]
+                        face = msg_ref[i, k - 1, j, span + 2]
                         face = ahead(face, x, 1) if x > 0 else face
                         plane = plane + jnp.where(lane == 0, face, 0.0)
                     target[1 + span * i + x, at_rows, at_lanes] = plane
                     if j > 0:
-                        face = msg_ref[block - counts[2], span + 1, x : x + 1, :]
+                        face = msg_ref[i, k, j - 1, span + 1, x : x + 1, :]
                         at_row = slice(rows * j, rows * j + 1)
                         target[1 + span * i + x, at_row, at_lanes] = (
                             target[1 + span * i + x, at_row, at_lanes] + face
@@ -793,20 +881,19 @@
             for y in range(rows):
                 upstream[d : d + 1, x * chunk + y * lanes : x * chunk + (y + 1) * lanes] = plane[y : y + 1]
     across = (((1,), (1,)), ((), ()))
-    hidden_size = win_ref.shape[0]
-    feat = win_ref.shape[1]
+    feat, hidden_size = win_ref.shape
     grad_in = jnp.zeros((feat, hidden_size), F32)
     grad_out = jnp.zeros((8, hidden_size), F32)
     grad_bias = jnp.zeros((8, hidden_size), F32)
     ones = jnp.ones((8, chunk), BF16)
     for x in range(span):
         columns = cols_ref[:, x * chunk : (x + 1) * chunk]
-        before = jnp.dot(win_ref[...], columns, preferred_element_type=F32) + bias_ref[...]
+        before = lax.dot_general(win_ref[...], columns, DOWN, preferred_element_type=F32) + bias_ref[...]
         gate = jax.nn.sigmoid(before)
         hidden = (before * gate).astype(BF16)
         up = upstream[:, x * chunk : (x + 1) * chunk].astype(BF16)
         grad_out = grad_out + lax.dot_general(up, hidden, across, preferred_element_type=F32)
-        grad_hidden = lax.dot_general(wout_ref[...], up, (((0,), (0,)), ((), ())), preferred_element_type=F32)
+        grad_hidden = jnp.dot(wout_ref[...], up[0:3], preferred_element_type=F32)
         grad_before = grad_hidden * (gate * (1.0 + before * (1.0 - gate)))
         high = grad_before.astype(BF16)
         low = (grad_before - high.astype(F32)).astype(BF16)
@@ -818,22 +905,90 @@
     out_ref[feat + 8 : feat + 16, :] = grad_bias
 
 
+def gather_kernel(counts, total, block_ref, *refs):
+    if total:
+        out_ref, all_ref, keep_sem, send_sem, recv_sem = refs
+    else:
+        all_ref, keep_sem, send_sem, recv_sem = refs
+    here = tuple(lax.axis_index(name) for name in AXES)
+
+    def peer(axis, shift):
+        where = list(here)
+        where[axis] = lax.rem(here[axis] + shift, counts[axis])
+        return tuple(where)
+
+    barrier = pltpu.get_barrier_semaphore()
+    for axis in range(3):
+        for shift in range(1, counts[axis]):
+            pl.semaphore_signal(barrier, inc=1, device_id=peer(axis, shift), device_id_type=pl.DeviceIdType.MESH)
+    keep = pltpu.make_async_copy(block_ref, all_ref.at[here[0], here[2], here[1]], keep_sem)
+    keep.start()
+    pl.semaphore_wait(barrier, sum(counts) - 3)
+    keep.wait()
+    slot = 0
+    for axis in (2, 0, 1):
+        part = {
+            2: all_ref.at[here[0], here[2], here[1]],
+            0: all_ref.at[here[0], :, here[1]],
+            1: all_ref.at[:, :, here[1]],
+        }[axis]
+        copies = []
+        for shift in range(1, counts[axis]):
+            copies.append(
+                pltpu.make_async_remote_copy(
+                    src_ref=part,
+                    dst_ref=part,
+                    send_sem=send_sem.at[slot],
+                    recv_sem=recv_sem.at[slot],
+                    device_id=peer(axis, shift),
+                    device_id_type=pl.DeviceIdType.MESH,
+                )
+            )
+            slot += 1
+        for copy in copies:
+            copy.start()
+        for copy in copies:
+            copy.wait()
+    if total:
+        result = jnp.zeros(out_ref.shape, F32)
+        for i in range(counts[0]):
+            for k in range(counts[2]):
+                for j in range(counts[1]):
+                    result = result + all_ref[i, k, j]
+        out_ref[...] = result
+
+
+def gather_blocks(block, counts, ident, total=False):
+    vmem = pl.BlockSpec(memory_space=pltpu.VMEM)
+    steps = sum(counts) - 3
+    every = (counts[0], counts[2], counts[1]) + block.shape
+    sems = [pltpu.SemaphoreType.DMA, pltpu.SemaphoreType.DMA((steps,)), pltpu.SemaphoreType.DMA((steps,))]
+    held = [pltpu.VMEM(every, F32)] if total else []
+    return pl.pallas_call(
+        functools.partial(gather_kernel, counts, total),
+        out_shape=jax.ShapeDtypeStruct(block.shape if total else every, F32),
+        in_specs=[vmem],
+        out_specs=vmem,
+        scratch_shapes=held + sems,
+        compiler_params=pltpu.CompilerParams(
+            collective_id=ident, has_side_effects=True, vmem_limit_bytes=VMEM_BYTES
+        ),
+        name="gather_" + str(ident),
+    )(block)
+
+
 def whole_device(counts, velocity, features, density, target, weight_in, bias_in, weight_out, open_faces):
-    axes = ("gx", "gy", "gz")
     shape = density.shape
     span, rows, lanes = shape
     whole = tuple(n * c for n, c in zip(shape, counts))
     feat, hidden_size = weight_in.shape
     cells = span * rows * lanes
-    opens = open_faces.astype(F32)
     columns = features.reshape(feat, cells)
-    win = weight_in.T
     bias = bias_in.reshape(hidden_size, 1)
-    wout = jnp.pad(weight_out.T, ((0, 5), (0, 0)))
     vmem = pl.BlockSpec(memory_space=pltpu.VMEM)
     smem = pl.BlockSpec(memory_space=pltpu.SMEM)
     params = pltpu.CompilerParams(vmem_limit_bytes=VMEM_BYTES)
-    blocks = lax.all_gather(density, axes, axis=0)
+    blocks = gather_blocks(density, counts, 1)
     field = jax.ShapeDtypeStruct((3,) + shape, F32)
     message = jax.ShapeDtypeStruct((span + 3, rows, lanes), F32)
     flux, msg = pl.pallas_call(
@@ -844,8 +999,8 @@
         scratch_shapes=[pltpu.VMEM((3,) + shape, F32)],
         compiler_params=params,
         name="closure_forward",
-    )(opens, columns, velocity, win, bias, wout)
-    sources = lax.all_gather(msg, axes, axis=0)
+    )(open_faces, columns, velocity, weight_in, bias, weight_out)
+    sources = gather_blocks(msg, counts, 2)
     padded = pltpu.VMEM((whole[0] + 2,) + whole[1:], F32)
     wide = pltpu.VMEM((6, span) + whole[1:], F32)
     scratch = [padded, padded, wide] + level_scratch(whole)
@@ -857,8 +1012,8 @@
         scratch_shapes=scratch,
         compiler_params=params,
         name="project",
-    )(opens, blocks, sources, flux, target)
-    sources = lax.all_gather(msg, axes, axis=0)
+    )(open_faces, blocks, sources, flux, target)
+    sources = gather_blocks(msg, counts, 3)
     sums = pl.pallas_call(
         functools.partial(adjoint_kernel, counts),
         out_shape=jax.ShapeDtypeStruct((feat + 16, hidden_size), F32),
@@ -867,8 +1022,8 @@
         scratch_shapes=[pltpu.VMEM((8, cells), F32)] + scratch,
         compiler_params=params,
         name="adjoint",
-    )(opens, blocks, sources, misfit, columns, win, bias, wout)
-    sums = lax.psum(sums, axes)
+    )(open_faces, blocks, sources, misfit, columns, weight_in, bias, weight_out)
+    sums = gather_blocks(sums, counts, 4, total=True)
     return new_velocity, sums[:feat], sums[feat + 8], sums[feat : feat + 3].T
 
 

time: 344 us -> 162 us (0.47)
  waiting for transfers between devices: 161 us -> 0 us
  blocking collectives: 39.2 us -> 0 us
  Pallas kernels: 121 us -> 152 us
  between operations: 13.7 us -> 0.67 us
    all_gather x3 -> x0, waiting for transfers between devices: 160 us -> none  [the longest x2 111 us: whole_device(): sources = lax.all_gather(msg, axes, axis=0)]
    pallas_call x0 -> x4, Pallas kernels: none -> 73 us  [gather_blocks(): pl.pallas_call(functools.partial(gather_kernel, counts, total), out_shape...]
    psum x1 -> x0, blocking collectives: 39.2 us -> none  [whole_device(): sums = lax.psum(sums, axes)]
    pallas_call x1, Pallas kernels: 59.6 us -> 38.7 us  [whole_device(): pl.pallas_call(functools.partial(adjoint_kernel, counts), out_shape=jax.S...]
    pallas_call x1, Pallas kernels: 57.8 us -> 37 us  [whole_device(): pl.pallas_call(functools.partial(project_kernel, counts), out_shape=(fiel...]
  transfers between devices with their start and end apart: 3 -> 0, of which waited for: 3 -> 0; matrix products, arithmetic and copies ran while one was open for 2% -> 0% of each run, Pallas kernels for 1% -> 0%
where the time goes in v2:
time: 162 us; the launch traced here: 161 us
  Pallas kernels  152 us (94%)
  local copies, waits for them, and re-layouts  8.3 us (5%)
    pallas_call x4, Pallas kernels, gather_blocks(): pl.pallas_call(functools.partial(gather_kernel, counts, total), out_shape...  73 us
    pallas_call x1, Pallas kernels, whole_device(): pl.pallas_call(functools.partial(adjoint_kernel, counts), out_shape=jax.S...  38.7 us
    pallas_call x1, Pallas kernels, whole_device(): pl.pallas_call(functools.partial(project_kernel, counts), out_shape=(fiel...  37 us
    pallas_call x1, Pallas kernels, whole_device(): pl.pallas_call(functools.partial(forward_kernel, counts), out_shape=(fiel...  3.32 us

profile of v2, /device:TPU:0, one launch (start us, length us, event | category | flops | bytes accessed | tf_op | source)
XLA Modules:
  0.0 161.0 jit_solution(7063978604193311682)
XLA Ops:
  0.6 1.4 copy.13.wout_ref
  2.0 1.4 copy.12.bias_ref
  3.4 1.8 %copy.18 = bf16[2,8,64,128]{3,1,2,0:T(8,128)(2,1)} copy(bf16[2,8,64,128]{3,2,1,0:T(8,128)(2,1)} %bitcast.12) | data formatting | bytes 524288
  5.2 3.3 %closure_forward.1 = (f32[3,8,8,128]{3,2,1,0:T(8,128)}, f32[11,8,128]{2,1,0:T(8,128)}) custom-call(s32[6]{0:T(128)} %open_ref.5, bf16[16,8192]{1,0:T(8,128)(2,1)} %bitcast.10, f32[3,8,8,128]{3,2,1,0:T(8,128)} %vel_ref.1, bf16[16,64]{1,0:T(8,128)(2,1)} %win_ref.3, f32[64,1]{1,0:T(8,128)} %copy.12.bias_ref, bf16[64,3]{1,0:T(8,128)(2,1)} %copy.13.wout_ref), custom_call_target="tpu_custom_call" | custom-call | tf_op jit(solution)/shard_map/closure_forward/pallas_call | solution.py:994
  8.5 18.6 %gather_1.1.density_ref = f32[4,4,2,8,8,128]{5,4,3,2,1,0:T(8,128)} custom-call(f32[8,8,128]{2,1,0:T(8,128)} %block_ref.1), custom_call_target="tpu_custom_call" | custom-call | tf_op jit(solution)/shard_map/gather_1/pallas_call | solution.py:967
  27.1 21.2 %gather_2.1.msg_ref = f32[4,4,2,11,8,128]{5,4,3,2,1,0:T(8,128)} custom-call(f32[11,8,128]{2,1,0:T(8,128)} %get-tuple-element.9.block_ref), custom_call_target="tpu_custom_call" | custom-call | tf_op jit(solution)/shard_map/gather_2/pallas_call | solution.py:967
  48.3 37.0 %project.1 = (f32[3,8,8,128]{3,2,1,0:T(8,128)}, f32[3,8,8,128]{3,2,1,0:T(8,128)}, f32[11,8,128]{2,1,0:T(8,128)}) custom-call(s32[6]{0:T(128)} %open_ref.5, f32[4,4,2,8,8,128]{5,4,3,2,1,0:T(8,128)} %gather_1.1.density_ref, f32[4,4,2,11,8,128]{5,4,3,2,1,0:T(8,128)} %gather_2.1.msg_ref, f32[3,8,8,128]{3,2,1,0:T(8,128)} %get-tuple-element.10.flux_ref, ...), custom_call_target="tpu_custom_call" | custom-call | tf_op jit(solution)/shard_map/project/pallas_call | solution.py:1007
  85.3 20.8 %gather_3.1.msg_ref = f32[4,4,2,11,8,128]{5,4,3,2,1,0:T(8,128)} custom-call(f32[11,8,128]{2,1,0:T(8,128)} %get-tuple-element.12.block_ref), custom_call_target="tpu_custom_call" | custom-call | tf_op jit(solution)/shard_map/gather_3/pallas_call | solution.py:967
  106.1 38.7 %adjoint.1.block_ref = f32[32,64]{1,0:T(8,128)} custom-call(s32[6]{0:T(128)} %open_ref.5, f32[4,4,2,8,8,128]{5,4,3,2,1,0:T(8,128)} %gather_1.1.density_ref, f32[4,4,2,11,8,128]{5,4,3,2,1,0:T(8,128)} %gather_3.1.msg_ref, f32[3,8,8,128]{3,2,1,0:T(8,128)} %get-tuple-element.13.misfit_ref, bf16[16,8192]{1,0:T(8,128)(2,1)} %bitcast.11, bf16[16,64]{1,0:T(8,128)(2,1)} %win_ref.3, ...), custom_call_target="tpu_custom_call" | custom-call | tf_op jit(solution)/shard_map/adjoint/pallas_call | solution.py:1017
  144.8 12.4 %gather_4.1 = f32[32,64]{1,0:T(8,128)} custom-call(f32[32,64]{1,0:T(8,128)} %adjoint.1.block_ref), custom_call_target="tpu_custom_call" | custom-call | tf_op jit(solution)/shard_map/gather_4/pallas_call | solution.py:967
  157.2 1.2 slice_bitcast_fusion.1
  158.4 1.3 slice_bitcast_fusion
  159.7 1.3 slice.9

commit v3 on v2

--- a/solution.py
+++ b/solution.py
@@ -420,7 +420,7 @@
 MSG = 11
 DOWN = (((0,), (0,)), ((), ()))
 AXES = ("gx", "gy", "gz")
-TILE = 128
+UNITS = (8, 128)
 VMEM_BYTES = 56 * 1024 * 1024
 
 
@@ -473,14 +473,14 @@
     return ends[0], second, third
 
 
-def forward_kernel(counts, open_ref, cols_ref, vel_ref, win_ref, bias_ref, wout_ref, flux_ref, msg_ref, corr):
+def forward_kernel(counts, open_ref, cols_ref, density_ref, vel_ref, win_ref, bias_ref, wout_ref, flux_ref, msg_ref, corr):
     _, span, rows, lanes = vel_ref.shape
     chunk = rows * lanes
     for x in range(span):
         before = lax.dot_general(win_ref[...], cols_ref[:, x * chunk : (x + 1) * chunk], DOWN, preferred_element_type=F32)
         before = before + bias_ref[...]
         hidden = (before * jax.nn.sigmoid(before)).astype(BF16)
-        out = lax.dot_general(wout_ref[...], hidden, DOWN, preferred_element_type=F32)
+        out = jnp.dot(wout_ref[...], hidden, preferred_element_type=F32)
         for d in range(3):
             for y in range(rows):
                 corr[d, x, y : y + 1, :] = out[d : d + 1, y * lanes : (y + 1) * lanes]
@@ -498,6 +498,7 @@
             planes.append(plane)
         fields.append(jnp.stack(planes))
     write_message(msg_ref, fields, -1.0)
+    msg_ref[span + 3 : 2 * span + 3] = density_ref[...]
 
 
 class Level:
@@ -511,108 +512,124 @@
     return total + jnp.dot(low, ones, preferred_element_type=F32)
 
 
-def pair_matrices(tools):
-    gather, spread = tools[0], tools[1]
-    for ref, fine, coarse in ((gather, 0, 1), (spread, 1, 0)):
-        hit = iota(ref.shape, fine) // 2 == iota(ref.shape, coarse)
-        ref[...] = jnp.where(hit, 1.0, 0.0).astype(BF16)
-
-
-def block_means(tools, span, plane_of, put):
-    gather, _, narrow, small, tall, _ = tools
-    half = tall.shape[2] // 2
-
-    def fold(x):
-        plane = plane_of(x)
-        for tile in range(tall.shape[1]):
-            at = slice(tile * TILE, (tile + 1) * TILE)
-            tall[x, tile] = plane[:, at]
-            even = tall[x, tile, pl.ds(0, half, stride=2), :]
-            odd = tall[x, tile, pl.ds(1, half, stride=2), :]
-            narrow[pl.ds(pl.multiple_of(x * half, half), half), at] = even + odd
-
-    loop(span, fold)
-    small[...] = exact_dot(narrow[...], gather[...]) * 0.125
-
-    def finish(x):
-        put(x, small[pl.ds(pl.multiple_of(x * half, half), half), :])
-
-    loop(span, finish)
-
-
-def copy_to_fine(tools, span, coarse, put):
-    _, spread, narrow, small, _, tall = tools
-    half = tall.shape[2] // 2
-
-    def pick(x):
-        small[pl.ds(pl.multiple_of(x * half, half), half), :] = coarse[x + 1]
-
-    loop(span, pick)
-    narrow[...] = exact_dot(small[...], spread[...])
-
-    def finish(x):
-        rows = narrow[pl.ds(pl.multiple_of(x * half, half), half), :]
-        for tile in range(tall.shape[1]):
-            part = rows[:, tile * TILE : (tile + 1) * TILE]
-            tall[x, tile, pl.ds(0, half, stride=2), :] = part
-            tall[x, tile, pl.ds(1, half, stride=2), :] = part
-        put(x, jnp.concatenate([tall[x, tile] for tile in range(tall.shape[1])], axis=1))
-
-    loop(span, finish)
-
-
-def pair_sum(plane, step):
-    rows, lanes = plane.shape
+def fold_matrices(tools):
+    px, pz, flat = tools
+    span, rows, lanes = flat.shape[0] - 2, flat.shape[1], flat.shape[2]
+    row = iota(px.shape, 0)
+    unit = lax.rem(row, span)
+    source = (lax.rem(unit, UNITS[0]) * (span // UNITS[0]) + unit // UNITS[0]) * rows + row // span
+    px[...] = jnp.where(source == iota(px.shape, 1), 1.0, 0.0).astype(BF16)
+    column = iota(pz.shape, 1)
+    source = lax.rem(column, UNITS[1]) * (lanes // UNITS[1]) + column // UNITS[1]
+    pz[...] = jnp.where(source == iota(pz.shape, 0), 1.0, 0.0).astype(BF16)
+
+
+def split_terms(values):
+    high = values.astype(BF16)
+    return high, (values - high.astype(F32)).astype(BF16)
+
+
+def to_folded(tools, target):
+    px, pz, flat = tools
+    span, rows, lanes = flat.shape[0] - 2, flat.shape[1], flat.shape[2]
+    values = exact_dot(flat[1 : span + 1].reshape(span * rows, lanes), pz[...])
+    terms = [jnp.dot(px[...], term, preferred_element_type=F32) for term in split_terms(values)]
+    target[1 : rows + 1] = (terms[0] + terms[1]).reshape(rows, span, lanes)
+
+
+def from_folded(tools, source):
+    px, pz, flat = tools
+    span, rows, lanes = flat.shape[0] - 2, flat.shape[1], flat.shape[2]
+    values = source[1 : rows + 1].reshape(rows * span, lanes)
+    across = (((1,), (1,)), ((), ()))
+    terms = [lax.dot_general(term, pz[...], across, preferred_element_type=F32) for term in split_terms(values)]
+    values = terms[0] + terms[1]
+    terms = [lax.dot_general(px[...], term, DOWN, preferred_element_type=F32) for term in split_terms(values)]
+    flat[1 : span + 1] = (terms[0] + terms[1]).reshape(span, rows, lanes)
+
+
+def part(plane, start, stop, dim):
+    return plane[start:stop, :] if dim == 0 else plane[:, start:stop]
+
+
+def join(parts, dim):
+    return parts[0] if len(parts) == 1 else jnp.concatenate(parts, axis=dim)
+
+
+def following(plane, dim):
+    unit, size = UNITS[dim], plane.shape[dim]
+    wrapped = pltpu.roll(part(plane, 0, unit, dim), unit - 1, dim)
+    return join(([part(plane, unit, size, dim)] if size > unit else []) + [wrapped], dim)
+
+
+def preceding(plane, dim):
+    unit, size = UNITS[dim], plane.shape[dim]
+    wrapped = pltpu.roll(part(plane, size - unit, size, dim), 1, dim)
+    return join([wrapped] + ([part(plane, 0, size - unit, dim)] if size > unit else []), dim)
+
+
+def pair_sum(plane):
+    for dim in (0, 1):
+        unit = UNITS[dim]
+        count = plane.shape[dim] // unit
+        pieces = [part(plane, n * unit, (n + 1) * unit, dim) for n in range(count)]
+        plane = join([pieces[n] + pieces[n + 1] for n in range(0, count, 2)], dim)
+    return plane
+
+
+def spread(plane):
+    for dim in (0, 1):
+        unit = UNITS[dim]
+        pieces = [part(plane, n * unit, (n + 1) * unit, dim) for n in range(plane.shape[dim] // unit)]
+        plane = join([piece for piece in pieces for twice in range(2)], dim)
+    return plane
+
+
+def raw_upper(flat_rho, open_ref, x):
+    rows, lanes = flat_rho.shape[1:]
     row = iota((rows, lanes), 0)
     lane = iota((rows, lanes), 1)
-    odd = lax.rem(row // step, 2) == 1
-    plane = plane + jnp.where(odd, behind(plane, step, 0), ahead(plane, step, 0))
-    odd = lax.rem(lane // step, 2) == 1
-    return plane + jnp.where(odd, behind(plane, step, 1), ahead(plane, step, 1))
-
-
-def raw_upper(level, open_ref, x):
-    rows, lanes = level.rho.shape[1:]
-    row = iota((rows, lanes), 0)
-    lane = iota((rows, lanes), 1)
-    step = level.step
-    rho = level.rho[x + 1]
+    step = 1
+    rho = flat_rho[x + 1]
     last_row = row >= rows - step
     last_lane = lane >= lanes - step
     one = jnp.float32(1.0)
-    up0 = jnp.where(x == level.span - 1, opened(open_ref, 1), one) * (2.0 * level.weight) / (rho + level.rho[x + 2])
-    up1 = (2.0 * level.weight) / (rho + jnp.where(last_row, 0.0, ahead(rho, step, 0)))
+    up0 = jnp.where(x == flat_rho.shape[0] - 3, opened(open_ref, 1), one) * (2.0) / (rho + flat_rho[x + 2])
+    up1 = (2.0) / (rho + jnp.where(last_row, 0.0, ahead(rho, step, 0)))
     up1 = up1 * jnp.where(last_row, opened(open_ref, 3), one)
-    up2 = (2.0 * level.weight) / (rho + jnp.where(last_lane, 0.0, ahead(rho, step, 1)))
+    up2 = (2.0) / (rho + jnp.where(last_lane, 0.0, ahead(rho, step, 1)))
     up2 = up2 * jnp.where(last_lane, opened(open_ref, 5), one)
     return up0, up1, up2
 
 
 def build_level(level, open_ref):
     rows, lanes = level.rho.shape[1:]
-    step = level.step
 
     def body(x, unused):
         row = iota((rows, lanes), 0)
         lane = iota((rows, lanes), 1)
         one = jnp.float32(1.0)
+        twice = 2.0 * level.weight
         rho = level.rho[x + 1]
-        up0, up1, up2 = raw_upper(level, open_ref, x)
-        twice = 2.0 * level.weight
-        down0 = jnp.where(x == 0, opened(open_ref, 0), one) * twice / (rho + level.rho[x])
-        first_row = row < step
-        first_lane = lane < step
-        down1 = jnp.where(first_row, opened(open_ref, 2) * twice / rho, behind(up1, step, 0))
-        down2 = jnp.where(first_lane, opened(open_ref, 4) * twice / rho, behind(up2, step, 1))
+        last_row, first_row = row == rows - 1, row == 0
+        last_lane, first_lane = lane == lanes - 1, lane == 0
+        up1 = jnp.where(x == level.span - 1, opened(open_ref, 3), one) * twice / (rho + level.rho[x + 2])
+        down1 = jnp.where(x == 0, opened(open_ref, 2), one) * twice / (rho + level.rho[x])
+        up0 = twice / (rho + jnp.where(last_row, 0.0, following(rho, 0)))
+        up2 = twice / (rho + jnp.where(last_lane, 0.0, following(rho, 1)))
+        down0 = jnp.where(first_row, opened(open_ref, 0) * twice / rho, preceding(up0, 0))
+        down2 = jnp.where(first_lane, opened(open_ref, 4) * twice / rho, preceding(up2, 1))
+        up0 = up0 * jnp.where(last_row, opened(open_ref, 1), one)
+        up2 = up2 * jnp.where(last_lane, opened(open_ref, 5), one)
         diagonal = MASS_SHIFT + up0 + down0 + up1 + down1 + up2 + down2
         scale = RELAXATION / diagonal
         level.scale[x] = scale
         level.unscale[x] = diagonal * (1.0 / RELAXATION)
-        level.coef[0, x] = scale * up0
-        level.coef[1, x] = scale * down0
-        level.coef[2, x] = jnp.where(row >= rows - step, 0.0, scale * up1)
-        level.coef[3, x] = jnp.where(first_row, 0.0, scale * down1)
-        level.coef[4, x] = jnp.where(lane >= lanes - step, 0.0, scale * up2)
+        level.coef[0, x] = scale * up1
+        level.coef[1, x] = scale * down1
+        level.coef[2, x] = jnp.where(last_row, 0.0, scale * up0)
+        level.coef[3, x] = jnp.where(first_row, 0.0, scale * down0)
+        level.coef[4, x] = jnp.where(last_lane, 0.0, scale * up2)
         level.coef[5, x] = jnp.where(first_lane, 0.0, scale * down2)
         return unused
 
@@ -620,12 +637,11 @@
 
 
 def smoothed(level, src, scaled, x):
-    step = level.step
     mid = src[x + 1]
     total = scaled[x + 1] + (1.0 - RELAXATION) * mid
     total = total + (level.coef[0, x] * src[x + 2] + level.coef[1, x] * src[x])
-    total = total + (level.coef[2, x] * ahead(mid, step, 0) + level.coef[3, x] * behind(mid, step, 0))
-    return total + (level.coef[4, x] * ahead(mid, step, 1) + level.coef[5, x] * behind(mid, step, 1))
+    total = total + (level.coef[2, x] * following(mid, 0) + level.coef[3, x] * preceding(mid, 0))
+    return total + (level.coef[4, x] * following(mid, 1) + level.coef[5, x] * preceding(mid, 1))
 
 
 def loop(count, body):
@@ -633,7 +649,7 @@
         body(x)
         return unused
 
-    lax.fori_loop(0, count, step, 0, unroll=4)
+    lax.fori_loop(0, count, step, 0, unroll=2)
 
 
 def sweep(level, src, dst, scaled):
@@ -666,20 +682,14 @@
     def store(x, mean):
         below.scaled[x + 1] = mean * below.scale[x]
 
-    if level.tools is not None:
-        block_means(level.tools, below.span, lower, store)
-    else:
-        loop(below.span, lambda x: store(x, pair_sum(lower(x), level.step) * 0.125))
+    loop(below.span, lambda x: store(x, pair_sum(lower(x)) * 0.125))
     coarse = cycle(levels[1:], below.scaled, below.one, below.two)
 
     def raise_(x, extra):
         src[2 * x + 1] = src[2 * x + 1] + extra
         src[2 * x + 2] = src[2 * x + 2] + extra
 
-    if level.tools is not None:
-        copy_to_fine(level.tools, below.span, coarse, raise_)
-    else:
-        loop(below.span, lambda x: raise_(x, coarse[x + 1]))
+    loop(below.span, lambda x: raise_(x, spread(coarse[x + 1])))
     for repeat in range(SWEEPS):
         sweep(level, src, dst, scaled)
         src, dst = dst, src
@@ -688,12 +698,11 @@
 
 def make_levels(refs):
     levels = []
-    tools = refs[:6]
-    refs = refs[6:]
+    tools = refs[:3]
+    refs = refs[3:]
     for depth in range(3):
         level = Level()
-        level.step = (1, 1, 2)[depth]
-        level.tools = tools if depth == 0 else None
+        level.tools = tools
         level.weight = 0.25**depth
         level.rho, level.scale, level.unscale, level.coef, level.scaled, level.one, level.two = refs[7 * depth : 7 * depth + 7]
         level.span = level.scale.shape[0]
@@ -702,18 +711,14 @@
 
 
 def level_scratch(whole):
-    span, rows, lanes = (whole[0] // 2, whole[1] // 2, whole[2] // 2)
     shapes = [
-        pltpu.VMEM((2 * lanes, lanes), BF16),
-        pltpu.VMEM((lanes, 2 * lanes), BF16),
-        pltpu.VMEM((span * rows, 2 * lanes), F32),
-        pltpu.VMEM((span * rows, lanes), F32),
-        pltpu.VMEM((span, 2 * lanes // TILE, 2 * rows, TILE), F32),
-        pltpu.VMEM((span, 2 * lanes // TILE, 2 * rows, TILE), F32),
+        pltpu.VMEM((whole[0] * whole[1],) * 2, BF16),
+        pltpu.VMEM((whole[2],) * 2, BF16),
+        pltpu.VMEM((whole[0] + 2,) + whole[1:], F32),
     ]
     for depth in range(3):
-        span = whole[0] // 2**depth
-        plane = tuple(whole[1:]) if depth == 0 else (whole[1] // 2, whole[2] // 2)
+        span = whole[1] // 2**depth
+        plane = (whole[0] // 2**depth, whole[2] // 2**depth)
         padded = pltpu.VMEM((span + 2,) + plane, F32)
         flat = pltpu.VMEM((span,) + plane, F32)
         shapes += [padded, flat, flat, pltpu.VMEM((6, span) + plane, F32), padded, padded, padded]
@@ -726,17 +731,24 @@
     ref[ref.shape[0] - 1] = zero
 
 
-def prepare(levels, open_ref, density_ref, counts):
-    span, rows, lanes = density_ref.shape[3:]
+def prepare(levels, open_ref, density_ref, counts, flat_rho):
+    span = (density_ref.shape[3] - 3) // 2
+    rows, lanes = density_ref.shape[4:]
+    flat = levels[0].tools[2]
+    clear_ends(flat_rho)
+    clear_ends(flat)
+    fold_matrices(levels[0].tools)
     for level in levels:
         for ref in (level.rho, level.scaled, level.one, level.two):
             clear_ends(ref)
     for i in range(counts[0]):
         for j in range(counts[1]):
             for k in range(counts[2]):
-                levels[0].rho[
+                flat_rho[
                     1 + span * i : 1 + span * (i + 1), rows * j : rows * (j + 1), lanes * k : lanes * (k + 1)
-                ] = density_ref[i, k, j]
+                ] = density_ref[i, k, j, span + 3 : 2 * span + 3]
+    flat[...] = flat_rho[...]
+    to_folded(levels[0].tools, levels[0].rho)
     for level, below in zip(levels[:-1], levels[1:]):
 
         def total(x, level=level):
@@ -745,18 +757,14 @@
         def store(x, mean, below=below):
             below.rho[x + 1] = mean
 
-        if level.tools is not None:
-            pair_matrices(level.tools)
-            block_means(level.tools, below.span, total, store)
-        else:
-            loop(below.span, lambda x: store(x, pair_sum(total(x), level.step) * 0.125))
+        loop(below.span, lambda x, total=total, store=store: store(x, pair_sum(total(x)) * 0.125))
     for level in levels:
         build_level(level, open_ref)
 
 
 def assemble(target, msg_ref, counts):
-    planes, rows, lanes = msg_ref.shape[3:]
-    span = planes - 3
+    rows, lanes = msg_ref.shape[4:]
+    span = (target.shape[0] - 2) // counts[0]
     lane = iota((rows, lanes), 1)
     for i in range(counts[0]):
         for j in range(counts[1]):
@@ -782,7 +790,9 @@
 
 def solve(levels, msg_ref, counts, kept):
     fine = levels[0]
-    assemble(fine.scaled, msg_ref, counts)
+    flat = fine.tools[2]
+    assemble(flat, msg_ref, counts)
+    to_folded(fine.tools, fine.scaled)
 
     def scale(x):
         fine.scaled[x + 1] = fine.scaled[x + 1] * fine.scale[x]
@@ -802,6 +812,8 @@
         kept[x + 1] = kept[x + 1] + second[x + 1]
 
     loop(fine.span, add)
+    from_folded(fine.tools, kept)
+    return flat
 
 
 def rises(kept, wide, slot, start, span):
@@ -825,20 +837,20 @@
     return wide[slot, :, pl.ds(pl.multiple_of(j * rows, rows), rows), pl.ds(pl.multiple_of(k * lanes, lanes), lanes)]
 
 
-def project_kernel(counts, open_ref, density_ref, msg_ref, flux_ref, target_ref, new_ref, misfit_ref, out_ref, kept, extra, wide, *refs):
+def project_kernel(counts, open_ref, density_ref, flux_ref, target_ref, new_ref, misfit_ref, out_ref, kept, extra, flat_rho, wide, *refs):
     levels = make_levels(refs)
     fine = levels[0]
     fine.again = extra
     clear_ends(kept)
     clear_ends(extra)
-    prepare(levels, open_ref, density_ref, counts)
-    solve(levels, msg_ref, counts, kept)
+    prepare(levels, open_ref, density_ref, counts, flat_rho)
+    flat = solve(levels, density_ref, counts, kept)
     _, span, rows, lanes = flux_ref.shape
     start = lax.axis_index("gx") * span
-    rises(kept, wide, 0, start, span)
+    rises(flat, wide, 0, start, span)
 
     def body(x, unused):
-        ups = raw_upper(fine, open_ref, start + x)
+        ups = raw_upper(flat_rho, open_ref, start + x)
         for d in range(3):
             wide[3 + d, x] = ups[d]
         return unused
@@ -856,17 +868,17 @@
     write_message(out_ref, fields, 1.0)
 
 
-def adjoint_kernel(counts, open_ref, density_ref, msg_ref, misfit_ref, cols_ref, win_ref, bias_ref, wout_ref, out_ref, upstream, kept, extra, wide, *refs):
+def adjoint_kernel(counts, open_ref, density_ref, msg_ref, misfit_ref, cols_ref, win_ref, bias_ref, wout_ref, out_ref, upstream, kept, extra, flat_rho, wide, *refs):
     levels = make_levels(refs)
     fine = levels[0]
     fine.again = extra
     clear_ends(kept)
     clear_ends(extra)
-    prepare(levels, open_ref, density_ref, counts)
-    solve(levels, msg_ref, counts, kept)
+    prepare(levels, open_ref, density_ref, counts, flat_rho)
+    flat = solve(levels, msg_ref, counts, kept)
     _, span, rows, lanes = misfit_ref.shape
     start = lax.axis_index("gx") * span
-    rises(kept, wide, 0, start, span)
+    rises(flat, wide, 0, start, span)
     first_end, second, third = local_outlets(open_ref, counts, (span, rows, lanes))
     chunk = rows * lanes
     upstream[...] = jnp.zeros(upstream.shape, F32)
@@ -893,7 +905,7 @@
         hidden = (before * gate).astype(BF16)
         up = upstream[:, x * chunk : (x + 1) * chunk].astype(BF16)
         grad_out = grad_out + lax.dot_general(up, hidden, across, preferred_element_type=F32)
-        grad_hidden = jnp.dot(wout_ref[...], up[0:3], preferred_element_type=F32)
+        grad_hidden = lax.dot_general(wout_ref[...], up[0:3], DOWN, preferred_element_type=F32)
         grad_before = grad_hidden * (gate * (1.0 + before * (1.0 - gate)))
         high = grad_before.astype(BF16)
         low = (grad_before - high.astype(F32)).astype(BF16)
@@ -988,32 +1000,32 @@
     vmem = pl.BlockSpec(memory_space=pltpu.VMEM)
     smem = pl.BlockSpec(memory_space=pltpu.SMEM)
     params = pltpu.CompilerParams(vmem_limit_bytes=VMEM_BYTES)
-    blocks = gather_blocks(density, counts, 1)
     field = jax.ShapeDtypeStruct((3,) + shape, F32)
     message = jax.ShapeDtypeStruct((span + 3, rows, lanes), F32)
     flux, msg = pl.pallas_call(
         functools.partial(forward_kernel, counts),
-        out_shape=(field, message),
-        in_specs=[smem] + [vmem] * 5,
+        out_shape=(field, jax.ShapeDtypeStruct((2 * span + 3, rows, lanes), F32)),
+        in_specs=[smem] + [vmem] * 6,
         out_specs=(vmem, vmem),
         scratch_shapes=[pltpu.VMEM((3,) + shape, F32)],
         compiler_params=params,
         name="closure_forward",
-    )(open_faces, columns, velocity, weight_in, bias, weight_out)
-    sources = gather_blocks(msg, counts, 2)
+    )(open_faces, columns, density, velocity, weight_in, bias, weight_out.T)
+    blocks = gather_blocks(msg, counts, 1)
     padded = pltpu.VMEM((whole[0] + 2,) + whole[1:], F32)
     wide = pltpu.VMEM((6, span) + whole[1:], F32)
-    scratch = [padded, padded, wide] + level_scratch(whole)
+    folded = pltpu.VMEM((whole[1] + 2, whole[0], whole[2]), F32)
+    scratch = [folded, folded, padded, wide] + level_scratch(whole)
     new_velocity, misfit, msg = pl.pallas_call(
         functools.partial(project_kernel, counts),
         out_shape=(field, field, message),
-        in_specs=[smem] + [vmem] * 4,
+        in_specs=[smem] + [vmem] * 3,
         out_specs=(vmem, vmem, vmem),
         scratch_shapes=scratch,
         compiler_params=params,
         name="project",
-    )(open_faces, blocks, sources, flux, target)
-    sources = gather_blocks(msg, counts, 3)
+    )(open_faces, blocks, flux, target)
+    sources = gather_blocks(msg, counts, 2)
     sums = pl.pallas_call(
         functools.partial(adjoint_kernel, counts),
         out_shape=jax.ShapeDtypeStruct((feat + 16, hidden_size), F32),
@@ -1022,8 +1034,8 @@
         scratch_shapes=[pltpu.VMEM((8, cells), F32)] + scratch,
         compiler_params=params,
         name="adjoint",
-    )(open_faces, blocks, sources, misfit, columns, weight_in, bias, weight_out)
-    sums = gather_blocks(sums, counts, 4, total=True)
+    )(open_faces, blocks, sources, misfit, columns, weight_in, bias, weight_out.T)
+    sums = gather_blocks(sums, counts, 3, total=True)
     return new_velocity, sums[:feat], sums[feat + 8], sums[feat : feat + 3].T
 
 

time: 162 us -> 136 us (0.84)
  Pallas kernels: 152 us -> 128 us
    pallas_call x1, Pallas kernels: 37 us -> 28.3 us  [whole_device(): pl.pallas_call(functools.partial(project_kernel, counts), out_shape=(fiel...]
    pallas_call x1, Pallas kernels: 38.7 us -> 30.6 us  [whole_device(): pl.pallas_call(functools.partial(adjoint_kernel, counts), out_shape=jax.S...]
    pallas_call x4 -> x3, Pallas kernels: 73 us -> 65.7 us  [gather_blocks(): pl.pallas_call(functools.partial(gather_kernel, counts, total), out_shape...]
where the time goes in v3:
time: 136 us; the launch traced here: 135 us
  Pallas kernels  128 us (94%)
  local copies, waits for them, and re-layouts  6.9 us (5%)
    pallas_call x3, Pallas kernels, gather_blocks(): pl.pallas_call(functools.partial(gather_kernel, counts, total), out_shape...  65.7 us
    pallas_call x1, Pallas kernels, whole_device(): pl.pallas_call(functools.partial(adjoint_kernel, counts), out_shape=jax.S...  30.6 us
    pallas_call x1, Pallas kernels, whole_device(): pl.pallas_call(functools.partial(project_kernel, counts), out_shape=(fiel...  28.3 us
    pallas_call x1, Pallas kernels, whole_device(): pl.pallas_call(functools.partial(forward_kernel, counts), out_shape=(fiel...  3.31 us

profile of v3, /device:TPU:0, one launch (start us, length us, event | category | flops | bytes accessed | tf_op | source)
XLA Modules:
  0.0 135.5 jit_solution(13845202893906557950)
XLA Ops:
  0.6 1.3 copy.12.bias_ref
  2.0 1.8 %copy.16 = bf16[2,8,64,128]{3,1,2,0:T(8,128)(2,1)} copy(bf16[2,8,64,128]{3,2,1,0:T(8,128)(2,1)} %bitcast.13) | data formatting | bytes 524288
  3.8 3.3 %closure_forward.1 = (f32[3,8,8,128]{3,2,1,0:T(8,128)}, f32[19,8,128]{2,1,0:T(8,128)}) custom-call(s32[6]{0:T(128)} %open_ref.5, bf16[16,8192]{1,0:T(8,128)(2,1)} %bitcast.11, f32[8,8,128]{2,1,0:T(8,128)} %density_ref.1, f32[3,8,8,128]{3,2,1,0:T(8,128)} %vel_ref.1, bf16[16,64]{1,0:T(8,128)(2,1)} %win_ref.3, f32[64,1]{1,0:T(8,128)} %copy.12.bias_ref, ...), custom_call_target="tpu_custom_call" | custom-call | tf_op jit(solution)/shard_map/closure_forward/pallas_call | solution.py:1005
  7.1 31.1 %gather_1.1.density_ref = f32[4,4,2,19,8,128]{5,4,3,2,1,0:T(8,128)} custom-call(f32[19,8,128]{2,1,0:T(8,128)} %get-tuple-element.9.block_ref), custom_call_target="tpu_custom_call" | custom-call | tf_op jit(solution)/shard_map/gather_1/pallas_call | solution.py:979
  38.2 28.3 %project.1 = (f32[3,8,8,128]{3,2,1,0:T(8,128)}, f32[3,8,8,128]{3,2,1,0:T(8,128)}, f32[11,8,128]{2,1,0:T(8,128)}) custom-call(s32[6]{0:T(128)} %open_ref.5, f32[4,4,2,19,8,128]{5,4,3,2,1,0:T(8,128)} %gather_1.1.density_ref, f32[3,8,8,128]{3,2,1,0:T(8,128)} %get-tuple-element.10.flux_ref, f32[3,8,8,128]{3,2,1,0:T(8,128)} %target_ref.1), custom_call_target="tpu_custom_call" | custom-call | tf_op jit(solution)/shard_map/project/pallas_call | solution.py:1019
  66.5 21.5 %gather_2.1.msg_ref = f32[4,4,2,11,8,128]{5,4,3,2,1,0:T(8,128)} custom-call(f32[11,8,128]{2,1,0:T(8,128)} %get-tuple-element.12.block_ref), custom_call_target="tpu_custom_call" | custom-call | tf_op jit(solution)/shard_map/gather_2/pallas_call | solution.py:979
  88.1 30.6 %adjoint.1.block_ref = f32[32,64]{1,0:T(8,128)} custom-call(s32[6]{0:T(128)} %open_ref.5, f32[4,4,2,19,8,128]{5,4,3,2,1,0:T(8,128)} %gather_1.1.density_ref, f32[4,4,2,11,8,128]{5,4,3,2,1,0:T(8,128)} %gather_2.1.msg_ref, f32[3,8,8,128]{3,2,1,0:T(8,128)} %get-tuple-element.13.misfit_ref, bf16[16,8192]{1,0:T(8,128)(2,1)} %bitcast.12, bf16[16,64]{1,0:T(8,128)(2,1)} %win_ref.3, ...), custom_call_target="tpu_custom_call" | custom-call | tf_op jit(solution)/shard_map/adjoint/pallas_call | solution.py:1029
  118.6 13.1 %gather_3.1 = f32[32,64]{1,0:T(8,128)} custom-call(f32[32,64]{1,0:T(8,128)} %adjoint.1.block_ref), custom_call_target="tpu_custom_call" | custom-call | tf_op jit(solution)/shard_map/gather_3/pallas_call | solution.py:979
  131.7 1.2 slice_bitcast_fusion.1
  132.9 1.3 slice_bitcast_fusion
  134.2 1.3 slice.9

commit v4 on v3

--- a/solution.py
+++ b/solution.py
@@ -937,30 +937,72 @@
     keep.start()
     pl.semaphore_wait(barrier, sum(counts) - 3)
     keep.wait()
-    slot = 0
-    for axis in (2, 0, 1):
-        part = {
-            2: all_ref.at[here[0], here[2], here[1]],
-            0: all_ref.at[here[0], :, here[1]],
-            1: all_ref.at[:, :, here[1]],
-        }[axis]
-        copies = []
-        for shift in range(1, counts[axis]):
-            copies.append(
-                pltpu.make_async_remote_copy(
-                    src_ref=part,
-                    dst_ref=part,
-                    send_sem=send_sem.at[slot],
-                    recv_sem=recv_sem.at[slot],
-                    device_id=peer(axis, shift),
-                    device_id_type=pl.DeviceIdType.MESH,
-                )
-            )
-            slot += 1
-        for copy in copies:
-            copy.start()
-        for copy in copies:
-            copy.wait()
+    slots = []
+
+    def send(back_x, back_z, axis, shift):
+        owner_x = lax.rem(here[0] + counts[0] - back_x, counts[0])
+        owner_z = lax.rem(here[2] + counts[2] - back_z, counts[2])
+        place = all_ref.at[owner_x, owner_z, here[1]]
+        slot = len(slots)
+        copy = pltpu.make_async_remote_copy(
+            src_ref=place,
+            dst_ref=place,
+            send_sem=send_sem.at[slot],
+            recv_sem=recv_sem.at[slot],
+            device_id=peer(axis, shift),
+            device_id_type=pl.DeviceIdType.MESH,
+        )
+        slots.append(copy)
+        copy.start()
+        return copy
+
+    def arrived(back_x, back_z, axis, shift, slot):
+        behind_x = back_x + (shift if axis == 0 else 0)
+        behind_z = back_z + (shift if axis == 2 else 0)
+        place = all_ref.at[
+            lax.rem(here[0] + counts[0] - behind_x, counts[0]),
+            lax.rem(here[2] + counts[2] - behind_z, counts[2]),
+            lax.rem(here[1] + shift, counts[1]) if axis == 1 else here[1],
+        ]
+        pltpu.make_async_remote_copy(
+            src_ref=place,
+            dst_ref=place,
+            send_sem=send_sem.at[slot],
+            recv_sem=recv_sem.at[slot],
+            device_id=peer(axis, shift),
+            device_id_type=pl.DeviceIdType.MESH,
+        ).wait_recv()
+
+    along_z = []
+    for shift in range(1, counts[2]):
+        along_z.append((shift, len(slots)))
+        send(0, 0, 2, shift)
+    along_x = []
+    along_y = []
+
+    def spread_plane(back_z):
+        for shift in range(1, counts[0]):
+            along_x.append((shift, back_z, len(slots)))
+            send(0, back_z, 0, shift)
+
+    def pass_over(back_x, back_z):
+        for shift in range(1, counts[1]):
+            along_y.append((back_x, back_z, shift, len(slots)))
+            send(back_x, back_z, 1, shift)
+
+    spread_plane(0)
+    pass_over(0, 0)
+    for shift, slot in along_z:
+        arrived(0, 0, 2, shift, slot)
+        spread_plane(shift)
+        pass_over(0, shift)
+    for shift, back_z, slot in along_x:
+        arrived(0, back_z, 0, shift, slot)
+        pass_over(shift, back_z)
+    for back_x, back_z, shift, slot in along_y:
+        arrived(back_x, back_z, 1, counts[1] - shift, slot)
+    for copy in slots:
+        copy.wait_send()
     if total:
         result = jnp.zeros(out_ref.shape, F32)
         for i in range(counts[0]):
@@ -972,7 +1014,7 @@
 
 def gather_blocks(block, counts, ident, total=False):
     vmem = pl.BlockSpec(memory_space=pltpu.VMEM)
-    steps = sum(counts) - 3
+    steps = counts[2] - 1 + counts[2] * (counts[0] - 1) + counts[0] * counts[2] * (counts[1] - 1)
     every = (counts[0], counts[2], counts[1]) + block.shape
     sems = [pltpu.SemaphoreType.DMA, pltpu.SemaphoreType.DMA((steps,)), pltpu.SemaphoreType.DMA((steps,))]
     held = [pltpu.VMEM(every, F32)] if total else []

time: 136 us -> 124 us (0.912)
  Pallas kernels: 128 us -> 116 us
    pallas_call x3, Pallas kernels: 65.7 us -> 53.4 us  [gather_blocks(): pl.pallas_call(functools.partial(gather_kernel, counts, total), out_shape...]
where the time goes in v4:
time: 124 us; the launch traced here: 123 us
  Pallas kernels  116 us (94%)
  local copies, waits for them, and re-layouts  6.9 us (6%)
    pallas_call x3, Pallas kernels, gather_blocks(): pl.pallas_call(functools.partial(gather_kernel, counts, total), out_shape...  53.4 us
    pallas_call x1, Pallas kernels, whole_device(): pl.pallas_call(functools.partial(adjoint_kernel, counts), out_shape=jax.S...  30.6 us
    pallas_call x1, Pallas kernels, whole_device(): pl.pallas_call(functools.partial(project_kernel, counts), out_shape=(fiel...  28.3 us
    pallas_call x1, Pallas kernels, whole_device(): pl.pallas_call(functools.partial(forward_kernel, counts), out_shape=(fiel...  3.31 us

profile of v4, /device:TPU:0, one launch (start us, length us, event | category | flops | bytes accessed | tf_op | source)
XLA Modules:
  0.0 123.2 jit_solution(15903450086487434640)
XLA Ops:
  0.6 1.3 %copy.12.bias_ref = f32[64,1]{1,0:T(8,128)} copy(f32[64,1]{0,1:T(1,128)} %bitcast.16) | data formatting | bytes 512 | tf_op jit(solution)/shard_map/reshape | solution.py:1041
  2.0 1.8 %copy.16 = bf16[2,8,64,128]{3,1,2,0:T(8,128)(2,1)} copy(bf16[2,8,64,128]{3,2,1,0:T(8,128)(2,1)} %bitcast.13) | data formatting | bytes 524288
  3.8 3.3 %closure_forward.1 = (f32[3,8,8,128]{3,2,1,0:T(8,128)}, f32[19,8,128]{2,1,0:T(8,128)}) custom-call(s32[6]{0:T(128)} %open_ref.5, bf16[16,8192]{1,0:T(8,128)(2,1)} %bitcast.11, f32[8,8,128]{2,1,0:T(8,128)} %density_ref.1, f32[3,8,8,128]{3,2,1,0:T(8,128)} %vel_ref.1, bf16[16,64]{1,0:T(8,128)(2,1)} %win_ref.3, f32[64,1]{1,0:T(8,128)} %copy.12.bias_ref, ...), custom_call_target="tpu_custom_call" | custom-call | tf_op jit(solution)/shard_map/closure_forward/pallas_call | solution.py:1047
  7.1 24.5 %gather_1.1.density_ref = f32[4,4,2,19,8,128]{5,4,3,2,1,0:T(8,128)} custom-call(f32[19,8,128]{2,1,0:T(8,128)} %get-tuple-element.9.block_ref), custom_call_target="tpu_custom_call" | custom-call | tf_op jit(solution)/shard_map/gather_1/pallas_call | solution.py:1021
  31.6 28.3 %project.1 = (f32[3,8,8,128]{3,2,1,0:T(8,128)}, f32[3,8,8,128]{3,2,1,0:T(8,128)}, f32[11,8,128]{2,1,0:T(8,128)}) custom-call(s32[6]{0:T(128)} %open_ref.5, f32[4,4,2,19,8,128]{5,4,3,2,1,0:T(8,128)} %gather_1.1.density_ref, f32[3,8,8,128]{3,2,1,0:T(8,128)} %get-tuple-element.10.flux_ref, f32[3,8,8,128]{3,2,1,0:T(8,128)} %target_ref.1), custom_call_target="tpu_custom_call" | custom-call | tf_op jit(solution)/shard_map/project/pallas_call | solution.py:1061
  59.9 16.8 %gather_2.1.msg_ref = f32[4,4,2,11,8,128]{5,4,3,2,1,0:T(8,128)} custom-call(f32[11,8,128]{2,1,0:T(8,128)} %get-tuple-element.12.block_ref), custom_call_target="tpu_custom_call" | custom-call | tf_op jit(solution)/shard_map/gather_2/pallas_call | solution.py:1021
  76.7 30.6 %adjoint.1.block_ref = f32[32,64]{1,0:T(8,128)} custom-call(s32[6]{0:T(128)} %open_ref.5, f32[4,4,2,19,8,128]{5,4,3,2,1,0:T(8,128)} %gather_1.1.density_ref, f32[4,4,2,11,8,128]{5,4,3,2,1,0:T(8,128)} %gather_2.1.msg_ref, f32[3,8,8,128]{3,2,1,0:T(8,128)} %get-tuple-element.13.misfit_ref, bf16[16,8192]{1,0:T(8,128)(2,1)} %bitcast.12, bf16[16,64]{1,0:T(8,128)(2,1)} %win_ref.3, ...), custom_call_target="tpu_custom_call" | custom-call | tf_op jit(solution)/shard_map/adjoint/pallas_call | solution.py:1071
  107.2 12.2 %gather_3.1 = f32[32,64]{1,0:T(8,128)} custom-call(f32[32,64]{1,0:T(8,128)} %adjoint.1.block_ref), custom_call_target="tpu_custom_call" | custom-call | tf_op jit(solution)/shard_map/gather_3/pallas_call | solution.py:1021
  119.4 1.2 slice_bitcast_fusion.1
  120.6 1.3 %slice_bitcast_fusion = f32[64,3]{0,1:T(4,128)} fusion(f32[32,64]{1,0:T(8,128)} %gather_3.1), kind=kLoop, calls=%fused_computation.1 | loop fusion | bytes 1536 | tf_op jit(solution)/shard_map/transpose | solution.py:1081
  121.9 1.3 %slice.9 = f32[16,64]{1,0:T(8,128)} slice(f32[32,64]{1,0:T(8,128)} %gather_3.1), slice={[0:16], [0:64]} | slice | bytes 8192 | tf_op jit(solution)/shard_map/slice | solution.py:1081
